TPU v7x, 32 devices: a whole 2x2x4 slice. The times are simulated.
32 devices in a mesh: dp: 8 (over y, x, core), freq: 4 (over z).
Axes of the slice: x: 2, y: 2, z: 4, core: 2. Of those that a mesh axis runs over, the one named last changes fastest.
Arguments:
- records: float32 [8, 2, 1024, 2048], P('dp', None, None, 'freq'), may hold values from -6 to 6
- stem_weight: bfloat16 [256, 512], replicated, may hold values from -0.375 to 0.375
- conv_weight: bfloat16 [3, 3, 16, 512], replicated, may hold values from -0.875 to 0.875
- mix_weight: bfloat16 [3, 512, 512], replicated, may hold values from -0.25 to 0.25
- head_weight: float32 [512, 10], replicated, may hold values from -0.25 to 0.25
- labels: int32 [8], P('dp'), may hold values from 0 to 9
- band_bounds: int32 [33], replicated, may hold values from 0 to 1048576, as said below
Outputs:
- loss: float32 [], replicated
- grad_stem: float32 [256, 512], replicated
- grad_conv: float32 [3, 3, 16, 512], replicated
- grad_mix: float32 [3, 512, 512], replicated
- grad_head: float32 [512, 10], replicated
Inputs may be any that keep to these rules, and one draw needn't show every extreme that they name: `band_bounds`: strictly increasing multiples of 128; the first is 0 and the last is half of 2097152.
All inputs are finite; a program needn't handle non-finite values.
Results may differ from a plain program's by a relative error of at most 0.0018.
Values may be sent and summed in bfloat16 or wider, within the bound.
No kernel may reach another device: no remote copies, remote signals or barrier semaphores. Data moves between devices by JAX's collectives and lax.ppermute only.
A program may use at most 192 MiB of HBM per device.

v0:
```python
import functools

import jax
import jax.numpy as jnp
import numpy as np
from jax import lax
from jax.experimental import pallas as pl
from jax.experimental.pallas import tpu as pltpu
from jax.sharding import PartitionSpec as P

POOL = 128
GROUP_WIDTH = 16
KW = 3
EPS = 1e-05
LANES = 128
HALF_MXU = 256
HALO = 16
TILE = 1024
F32 = jnp.float32
BF16 = jnp.bfloat16


def split16(values):
    high = values.astype(BF16)
    return high, (values - high.astype(F32)).astype(BF16)


def table_pair(values):
    high = values.astype(jnp.bfloat16)
    return np.stack([high, (values - high.astype(np.float64)).astype(jnp.bfloat16)])


def first_tables(first_len, second_len):
    total_len = first_len * second_len
    rows = np.arange(first_len // 2)
    odd = 2 * rows + 1
    angles = (np.outer(np.arange(first_len), odd) % (2 * first_len)) * (np.pi / first_len)
    twiddles = (np.outer(np.arange(second_len), odd) % (2 * total_len)) * (np.pi / total_len)

    def by_block(a, b):
        blocks = first_len // 2 // LANES
        a = a.reshape(a.shape[0], blocks, 1, LANES)
        b = b.reshape(b.shape[0], blocks, 1, LANES)
        return np.concatenate([a, b], axis=2).reshape(a.shape[0], -1)

    section = table_pair(by_block(np.cos(angles), -np.sin(angles)))
    twiddle = by_block(np.cos(twiddles), np.sin(twiddles)).astype(np.float32)
    return section, twiddle


def second_tables(second_len):
    quarter = second_len // 4
    idx = np.arange(quarter)
    angles = np.outer(np.arange(1, 4), idx) * (2 * np.pi / second_len)
    spread = np.stack([np.cos(angles), np.sin(angles)], axis=1)[..., None] * np.ones(LANES)
    order = np.concatenate([idx[: quarter // 2], idx[quarter // 2 :][::-1]])
    inner = (np.outer(order, idx) % quarter) * (2 * np.pi / quarter)
    table = table_pair(np.concatenate([np.cos(inner), np.sin(inner)], axis=1))
    flip = np.eye(LANES)[::-1].astype(jnp.bfloat16)
    return spread.astype(np.float32), table, flip


def level_of(exponent, mantissa):
    return mantissa * jnp.exp(exponent * np.log(2.0).astype(np.float32)) * (1.0 / (16384.0 * 32767.0))


def first_kernel(devices, place_ref, x_ref, table_ref, twiddle_ref, *refs):
    outs, (highs, lows, codes) = refs[:devices], refs[devices:]
    signals, cols, _ = highs.shape
    block = pl.program_id(0)

    @pl.when(block == 0)
    def _():
        for signal in range(signals):
            highs[signal], lows[signal] = split16(x_ref[signal].T)

    row = lax.broadcasted_iota(jnp.int32, (HALO, 2 * LANES), 0)
    cosine, sine = twiddle_ref[:, :LANES], twiddle_ref[:, LANES:]
    for signal in range(signals):
        both = jnp.dot(highs[signal], table_ref[0], preferred_element_type=F32)
        both += jnp.dot(lows[signal], table_ref[0], preferred_element_type=F32)
        both += jnp.dot(highs[signal], table_ref[1], preferred_element_type=F32)
        real, imag = both[:, :LANES], both[:, LANES:]
        turned = jnp.concatenate(
            [real * cosine + imag * sine, imag * cosine - real * sine], axis=1
        )
        top = jnp.maximum(jnp.max(jnp.abs(turned), axis=0, keepdims=True), 1e-20)
        exponent = jnp.ceil(jnp.log(top) * (1.0 / np.log(2.0)))
        mantissa = jnp.floor(
            top * jnp.exp(-exponent * np.log(2.0).astype(np.float32)) * 16384.0
        ) + 1.0
        level = 1.0 / level_of(exponent, mantissa)
        codes[:cols, :] = jnp.round(turned * level).astype(jnp.int32).astype(jnp.int16)
        head = jnp.where(row == 0, exponent, jnp.where(row == 1, mantissa, 0.0))
        codes[cols:, :] = head.astype(jnp.int32).astype(jnp.int16)
        for shift in range(devices):

            @pl.when((place_ref[0] + shift) % devices == block * signals + signal)
            def _(shift=shift):
                outs[shift][...] = codes[...]


def first_section(place, records, at, signals, devices, section, twiddle):
    first_len, cols = records.shape[-2:]
    blocks = devices // signals
    shape = (cols + HALO, 2 * LANES)
    return pl.pallas_call(
        functools.partial(first_kernel, devices),
        out_shape=[jax.ShapeDtypeStruct(shape, jnp.int16)] * devices,
        grid_spec=pltpu.PrefetchScalarGridSpec(
            num_scalar_prefetch=1,
            grid=(blocks,),
            in_specs=[
                pl.BlockSpec((signals, first_len, cols), lambda i, s: (at, 0, 0)),
                pl.BlockSpec((2, first_len, 2 * LANES), lambda i, s: (0, 0, i)),
                pl.BlockSpec((cols, 2 * LANES), lambda i, s: (s[0], i)),
            ],
            out_specs=[pl.BlockSpec(shape, lambda i, s: (0, 0))] * devices,
            scratch_shapes=[
                pltpu.VMEM((signals, cols, first_len), BF16),
                pltpu.VMEM((signals, cols, first_len), BF16),
                pltpu.VMEM(shape, jnp.int16),
            ],
        ),
        compiler_params=pltpu.CompilerParams(vmem_limit_bytes=60 * 1024 * 1024),
        cost_estimate=pl.CostEstimate(
            flops=6 * signals * first_len * first_len * cols, bytes_accessed=2**23, transcendentals=0
        ),
        name="first_section",
    )(place, records, section, twiddle)


def second_kernel(devices, total_len, place_ref, *refs):
    received, refs = refs[:devices], refs[devices:]
    (spread_ref, table_ref, flip_ref), refs = refs[:3], refs[3:]
    outs, (signal, right, rest, packed) = refs[:devices], refs[devices:]
    place = place_ref[0]
    cols = signal.shape[0] // devices
    quarter = signal.shape[0] // 4
    run = quarter // 2 // devices
    for shift in range(devices):
        source = (place - shift + devices) % devices
        head = received[shift][cols:, :].astype(jnp.int32).astype(F32)
        values = received[shift][:cols, :].astype(jnp.int32).astype(F32)
        rows = pl.ds(pl.multiple_of(source * cols, cols), cols)
        signal[rows, :] = values * level_of(head[0:1], head[1:2])
    step = min(quarter, 128)
    for at in range(0, quarter, step):
        parts = [signal[g * quarter + at : g * quarter + at + step, :] for g in range(4)]
        re = [v[:, :LANES] for v in parts]
        im = [v[:, LANES:] for v in parts]
        sum_r, dif_r = re[0] + re[2], re[0] - re[2]
        sum_i, dif_i = im[0] + im[2], im[0] - im[2]
        odd_r, odm_r = re[1] + re[3], re[1] - re[3]
        odd_i, odm_i = im[1] + im[3], im[1] - im[3]
        turned = [
            (sum_r + odd_r, sum_i + odd_i),
            (dif_r + odm_i, dif_i - odm_r),
            (sum_r - odd_r, sum_i - odd_i),
            (dif_r - odm_i, dif_i + odm_r),
        ]
        for c in range(4):
            real, imag = turned[c]
            if c:
                cosine = spread_ref[c - 1, 0, at : at + step, :]
                sine = spread_ref[c - 1, 1, at : at + step, :]
                real, imag = real * cosine + imag * sine, imag * cosine - real * sine
            first = slice(2 * LANES * c, 2 * LANES * c + LANES)
            second = slice(2 * LANES * c + LANES, 2 * LANES * (c + 1))
            for ref, r, i in zip((right, rest), split16(real), split16(imag)):
                ref[at : at + step, first] = r
                ref[at : at + step, second] = i
                ref[quarter + at : quarter + at + step, first] = i
                ref[quarter + at : quarter + at + step, second] = -r
    row = lax.broadcasted_iota(jnp.int32, (HALO, LANES), 0)
    edges = [jnp.zeros((HALO, LANES), F32) for _ in range(devices)]
    for c in range(4):
        lanes = slice(2 * LANES * c, 2 * LANES * (c + 1))
        both = jnp.dot(table_ref[0], right[:, lanes], preferred_element_type=F32)
        both += jnp.dot(table_ref[0], rest[:, lanes], preferred_element_type=F32)
        both += jnp.dot(table_ref[1], right[:, lanes], preferred_element_type=F32)
        power = both[:, :LANES] ** 2 + both[:, LANES:] ** 2
        features = jnp.log1p(power * (1.0 / total_len))
        low = features[: quarter // 2].astype(BF16)
        high = jnp.dot(
            features[quarter // 2 :].astype(BF16), flip_ref[...], preferred_element_type=F32
        )
        for part, values, group in ((0, low, c), (1, high.astype(BF16), 4 + 3 - c)):
            wide = values.astype(F32)
            for to in range(devices):
                packed[to, group * run : (group + 1) * run, :] = values[to * run : (to + 1) * run]
                if group % 4 == 3 and to > 0:
                    edges[to] = jnp.where(
                        row == 2 * part, wide[to * run - 1 : to * run], edges[to]
                    )
                if group % 4 == 0 and to < devices - 1:
                    edges[to] = jnp.where(
                        row == 2 * part + 1, wide[(to + 1) * run : (to + 1) * run + 1], edges[to]
                    )
    for to in range(devices):
        packed[to, 8 * run :, :] = edges[to].astype(BF16)
    for shift in range(devices):
        outs[shift][...] = packed[(place + shift) % devices]


def second_section(place, received, second_len, total_len, spread, table, flip):
    devices = len(received)
    quarter = second_len // 4
    run = quarter // 2 // devices
    shape = (8 * run + HALO, LANES)
    vmem = pl.BlockSpec(memory_space=pltpu.VMEM)
    return pl.pallas_call(
        functools.partial(second_kernel, devices, total_len),
        out_shape=[jax.ShapeDtypeStruct(shape, BF16)] * devices,
        in_specs=[pl.BlockSpec(memory_space=pltpu.SMEM)] + [vmem] * (devices + 3),
        out_specs=[vmem] * devices,
        scratch_shapes=[
            pltpu.VMEM((second_len, 2 * LANES), F32),
            pltpu.VMEM((2 * quarter, 8 * LANES), BF16),
            pltpu.VMEM((2 * quarter, 8 * LANES), BF16),
            pltpu.VMEM((devices,) + shape, BF16),
        ],
        compiler_params=pltpu.CompilerParams(vmem_limit_bytes=32 * 1024 * 1024),
        cost_estimate=pl.CostEstimate(
            flops=96 * LANES * quarter * quarter, bytes_accessed=2**23, transcendentals=0
        ),
        name="second_section",
    )(place, *received, spread, table, flip)


def position_column(start, run, at, rows):
    row = at + lax.broadcasted_iota(jnp.int32, (rows, 1), 0)
    return start + row // run + 32 * (row % run)


def halo_column(start, count):
    row = lax.broadcasted_iota(jnp.int32, (HALO, 1), 0)
    return start + jnp.where(row < 8, row - 8, count + row - 8)


def silu_gate(v):
    return 0.5 + 0.5 * jnp.tanh(0.5 * v)


def close_ends(padded, halo, run):
    count = padded.shape[0] - 2 * run - HALO
    row = lax.broadcasted_iota(jnp.int32, (run, 1), 0)
    tail = padded[count : count + run, :].astype(F32)
    head = padded[run : 2 * run, :].astype(F32)
    before = jnp.where(row == 0, halo[7:8], pltpu.roll(tail, 1, 0))
    after = jnp.where(row == run - 1, halo[8:9], pltpu.roll(head, run - 1, 0))
    padded[:run, :] = before.astype(BF16)
    padded[run + count : 2 * run + count, :] = after.astype(BF16)
    padded[2 * run + count :, :] = halo.astype(BF16)
    row = lax.broadcasted_iota(jnp.int32, (HALO, 1), 0)
    down = jnp.where(row == 8, tail[run - 1 : run], pltpu.roll(halo, 1, 0))
    up = jnp.where(row == 7, head[:1], pltpu.roll(halo, HALO - 1, 0))
    return [v.astype(BF16) for v in (down, halo, up)]


def taps_product(windows, kernels):
    halves = []
    for half in range(kernels.shape[0]):
        lanes = slice(half * HALF_MXU, (half + 1) * HALF_MXU)
        total = None
        for tap in range(KW):
            term = jnp.dot(
                windows[tap](lanes), kernels[half, tap], preferred_element_type=F32
            )
            total = term if total is None else total + term
        halves.append(total)
    return jnp.concatenate(halves, axis=1)


def forward_kernel(run, devices, chunks, place_ref, *refs):
    received, refs = refs[: chunks * devices], refs[chunks * devices :]
    (stem_in, kernels_in, mix_in, bounds, preacts_out, scales_out, padded_out, feats_out, partial_out,
     preacts, scales, padded, feats, stem, kernels, mix, stream, halos, sems, sems_in, sems_tile) = refs
    layers = mix.shape[0]
    weights = [pltpu.make_async_copy(stem_in, stem, sems_in.at[0])]
    for layer in range(layers):
        for k, (src, dst) in enumerate(((kernels_in, kernels), (mix_in, mix))):
            weights.append(
                pltpu.make_async_copy(src.at[layer], dst.at[layer], sems_in.at[1 + 2 * layer + k])
            )
    for copy in weights:
        copy.start()
    count = 32 * run
    place = place_ref[0]
    start = place * count
    signals = 2 // chunks
    blocks = devices // signals

    row16 = lax.broadcasted_iota(jnp.int32, (HALO, LANES), 0)
    edge = [jnp.zeros((HALO, LANES), F32) for _ in range(2)]
    for chunk in range(chunks):
        for shift in range(devices):
            ref = received[chunk * devices + shift]
            source = (place - shift + devices) % devices
            ends = ref[8 * run :, :].astype(F32)
            channel = chunk if chunks == 2 else source % 2
            lanes = pl.ds(pl.multiple_of(channel * LANES, LANES), LANES)
            for part in range(2):
                block = source // signals
                block = 2 * blocks - 1 - block if part else block
                for c in range(4):
                    at = pl.multiple_of((block + 8 * c) * run, run)
                    feats[pl.ds(at, run), lanes] = ref[
                        (part * 4 + c) * run : (part * 4 + c + 1) * run, :
                    ]
                for which in range(2):
                    value = ends[2 * part + which : 2 * part + which + 1]
                    at = row16 == block + 8 * which
                    for k in range(2):
                        edge[k] = jnp.where(at & (channel == k), value, edge[k])
    for k in range(2):
        feats[count:, k * LANES : (k + 1) * LANES] = edge[k].astype(BF16)
    copies = []

    saved = []

    def save(source, target):
        copy = pltpu.make_async_copy(source, target, sems.at[len(saved)])
        copy.start()
        saved.append(copy)

    save(feats, feats_out)
    halo_place = halo_column(start, count)
    inside = ((halo_place >= 0) & (halo_place < devices * count)).astype(F32)
    tile = min(TILE, count)

    def norm(layer, rows, values):
        scale = lax.rsqrt(jnp.mean(values * values, axis=-1, keepdims=True) + EPS)
        scales[layer, rows, :] = jnp.broadcast_to(scale, (values.shape[0], LANES))
        return values * scale

    def put_normed(layer, at, values):
        normed = norm(layer, pl.ds(at, tile), values)
        padded[layer, pl.ds(pl.multiple_of(at + run, run), tile), :] = normed.astype(BF16)

    def stem_tile(i, _):
        at = pl.multiple_of(i * tile, tile)
        values = jnp.dot(feats[pl.ds(at, tile), :], stem[...], preferred_element_type=F32)
        stream[pl.ds(at, tile), :] = values
        put_normed(0, at, values)
        return 0

    weights[0].wait()
    lax.fori_loop(0, count // tile, stem_tile, 0)
    values = jnp.dot(feats[count:, :], stem[...], preferred_element_type=F32)
    stream[count:, :] = values
    halos[...] = norm(0, slice(count, count + HALO), values) * inside
    partial_out[...] = jnp.zeros_like(partial_out)

    for layer in range(layers):
        here = padded.at[layer]
        windows = close_ends(here, halos[...].astype(BF16).astype(F32), run)
        save(here, padded_out.at[layer])
        save(scales.at[layer], scales_out.at[layer])
        last = layer == layers - 1
        weights[1 + 2 * layer].wait()
        weights[2 + 2 * layer].wait()

        def save_tile(i, layer=layer):
            rows = pl.ds(pl.multiple_of(i * tile, tile), tile)
            return pltpu.make_async_copy(
                preacts.at[layer, rows, :], preacts_out.at[layer, rows, :], sems_tile.at[layer, i]
            )

        def layer_tile(i, _, layer=layer, here=here, last=last, save_tile=save_tile):
            at = pl.multiple_of(i * tile, tile)
            rows = pl.ds(at, tile)
            taps = [
                lambda lanes, t=t: here[pl.ds(pl.multiple_of(at + t * run, run), tile), lanes]
                for t in range(KW)
            ]
            preact = taps_product(taps, kernels.at[layer])
            preacts[layer, rows, :] = preact
            save_tile(i).start()
            active = (preact * silu_gate(preact)).astype(BF16)
            values = stream[rows, :] + jnp.dot(active, mix[layer], preferred_element_type=F32)
            if last:
                place = position_column(start, run, at, tile)
                member = (place >= bounds[0:1, :]) & (place < bounds[1:2, :])
                kept = jnp.where(member, values, 0.0)
                partial_out[...] += jnp.sum(kept.reshape(tile // 8, 8, kept.shape[1]), axis=0)
            else:
                stream[rows, :] = values
                put_normed(layer + 1, at, values)
            return 0

        lax.fori_loop(0, count // tile, layer_tile, 0)
        preact = taps_product([lambda lanes, v=v: v[:, lanes] for v in windows], kernels.at[layer])
        preacts[layer, count:, :] = preact
        rest = pl.ds(count, HALO)
        save(preacts.at[layer, rest, :], preacts_out.at[layer, rest, :])
        copies.extend(save_tile(i) for i in range(count // tile))
        if not last:
            active = (preact * silu_gate(preact)).astype(BF16)
            values = stream[count:, :] + jnp.dot(active, mix[layer], preferred_element_type=F32)
            stream[count:, :] = values
            halos[...] = norm(layer + 1, slice(count, count + HALO), values) * inside
    for copy in saved + copies:
        copy.wait()


def backward_kernel(run, devices, all_records, place_ref, *refs):
    sums, refs = refs[:devices], refs[devices:]
    (preacts_in, scales_in, padded_in, feats_in, bounds, head, kernels_in, mix_in, kept, sent,
     preacts, scales, padded, feats, kernels, mix_t, sums_out, grad, ahead, active_t, out16,
     sems, sems_out) = refs
    layers = mix_t.shape[0]
    channels = grad.shape[1]
    count = 32 * run
    start = place_ref[0] * count
    core = place_ref[3]
    tile = min(TILE, count)
    tiles = count // tile

    arriving = []
    for layer in reversed(range(layers)):
        cuts = [pl.ds(k * tile, tile) for k in range(tiles)] + [pl.ds(count, HALO)]
        copies = [(preacts_in.at[layer, cut, :], preacts.at[layer, cut, :]) for cut in cuts]
        copies += [(padded_in.at[layer], padded.at[layer]), (scales_in.at[layer], scales.at[layer])]
        copies += [(kernels_in.at[layer], kernels.at[layer])]
        copies = [(mix_in.at[layer], mix_t.at[layer])] + copies
        arriving.append(copies)
    arriving.append([(feats_in, feats)])
    at = 0
    for k, copies in enumerate(arriving):
        arriving[k] = [
            pltpu.make_async_copy(*copy, sems.at[at + j]) for j, copy in enumerate(copies)
        ]
        at += len(copies)
        for copy in arriving[k]:
            copy.start()

    half_rows = kept.shape[0]
    leaving = []

    def put(at, value):
        sums_out[at : at + value.shape[0], :] = value

    def leave(at, rows):
        half, to = divmod(at, half_rows)
        source, sem = sums_out.at[pl.ds(at, rows), :], sems_out.at[len(leaving)]
        to = pl.ds(to, rows)
        leaving.append(pltpu.make_async_copy(source, kept.at[to, :], sem))

        @pl.when(core == half)
        def _():
            pltpu.make_async_copy(source, kept.at[to, :], sem).start()

        @pl.when(core != half)
        def _():
            pltpu.make_async_copy(source, sent.at[to, :], sem).start()

    total = sums[0][...]
    for ref in sums[1:]:
        total = total + ref[...]
    band_sum = jnp.sum(total, axis=0, keepdims=True)
    counts = (bounds[1:2, :] - bounds[0:1, :]).astype(F32)
    pooled = band_sum / counts
    row = lax.broadcasted_iota(jnp.int32, (HALO, 1), 0)
    logits = jnp.sum(head[...] * pooled, axis=1, keepdims=True)
    exponents = jnp.where(row < place_ref[2], jnp.exp(logits), 0.0)
    denominator = jnp.sum(exponents, axis=0, keepdims=True)
    one_hot = (row == place_ref[1]).astype(F32)
    loss = jnp.log(denominator) - jnp.sum(one_hot * logits, axis=0, keepdims=True)
    loss = loss / all_records
    grad_logits = (exponents / denominator - one_hot) / all_records
    grad_pooled = jnp.sum(head[...] * grad_logits, axis=0, keepdims=True)
    grad_band = grad_pooled / counts
    lead = (place_ref[0] == 0).astype(F32)
    stem_at = layers * channels
    conv_at = stem_at + 2 * LANES
    head_at = conv_at + layers * KW * GROUP_WIDTH
    put(head_at, lead * jnp.where(row == HALO - 1, loss, grad_logits * pooled))
    rest = 2 * half_rows - head_at - HALO
    if rest:
        put(head_at + HALO, jnp.zeros((rest, channels), F32))

    def spread(place):
        member = (place >= bounds[0:1, :]) & (place < bounds[1:2, :])
        return jnp.where(member, grad_band, 0.0)

    halo_place = halo_column(start, count)
    inside = ((halo_place >= 0) & (halo_place < devices * count)).astype(F32)
    grad[count:, :] = spread(halo_place)

    def gate_grad(value, grad_act):
        gate = silu_gate(value)
        return grad_act * gate * (1.0 + value * (1.0 - gate)), value * gate

    def stream_grad(layer, outgoing, rows, normed, grad_normed):
        scale = jnp.concatenate([scales[layer, rows, :]] * (channels // LANES), axis=1)
        normed = normed.astype(F32)
        inner = jnp.mean(normed * grad_normed, axis=-1, keepdims=True)
        return outgoing + scale * (grad_normed - normed * inner)

    at_row = lax.broadcasted_iota(jnp.int32, (HALF_MXU, HALF_MXU), 0) // GROUP_WIDTH
    at_col = lax.broadcasted_iota(jnp.int32, (HALF_MXU, HALF_MXU), 1) // GROUP_WIDTH
    for layer in reversed(range(layers)):
        copies = arriving[layers - 1 - layer]
        top, bottom = layer == layers - 1, layer == 0

        def act_tile(i, _, layer=layer, top=top):
            at = pl.multiple_of(i * tile, tile)
            rows = pl.ds(at, tile)
            if top:
                values = spread(position_column(start, run, at, tile))
                grad[rows, :] = values
            else:
                values = grad[rows, :]
            outgoing = values.astype(BF16)
            out16[rows, :] = outgoing
            grad_act = jnp.dot(outgoing, mix_t[layer], preferred_element_type=F32)
            grad_pre, act = gate_grad(preacts[layer, rows, :], grad_act)
            grad_pre = grad_pre.astype(BF16)
            active_t[:, rows] = act.astype(BF16).T
            ahead[pl.ds(pl.multiple_of(at + run, run), tile), :] = grad_pre
            return 0

        copies[0].wait()
        if top:
            for k in range(tiles):
                copies[1 + k].wait()
                lax.fori_loop(k, k + 1, act_tile, 0)
        else:
            for k in range(tiles):
                copies[1 + k].wait()
            lax.fori_loop(0, tiles, act_tile, 0)
        copies[1 + tiles].wait()
        grad_act = jnp.dot(grad[count:, :].astype(BF16), mix_t[layer], preferred_element_type=F32)
        halo, _ = gate_grad(preacts[layer, count:, :], grad_act)
        halo = (halo * inside).astype(BF16).astype(F32)
        windows = close_ends(ahead, halo, run)

        put(
            layer * channels,
            jnp.dot(active_t[...], out16[...], preferred_element_type=F32),
        )
        leave(layer * channels, channels)

        copies[tiles + 2].wait()
        for tap in range(KW):
            folded = []
            for half in range(channels // HALF_MXU):
                lanes = slice(half * HALF_MXU, (half + 1) * HALF_MXU)
                full = lax.dot_general(
                    padded[layer, tap * run : tap * run + count, lanes],
                    ahead[run : run + count, lanes],
                    (((0,), (0,)), ((), ())),
                    preferred_element_type=F32,
                )
                full = jnp.where(at_row == at_col, full, 0.0)
                folded.append(
                    jnp.sum(full.reshape(HALF_MXU // GROUP_WIDTH, GROUP_WIDTH, HALF_MXU), axis=0)
                )
            at = conv_at + (layer * KW + tap) * GROUP_WIDTH
            put(at, jnp.concatenate(folded, axis=1))
        copies[tiles + 3].wait()
        copies[tiles + 4].wait()

        def stream_tile(i, _, layer=layer, bottom=bottom):
            at = pl.multiple_of(i * tile, tile)
            rows = pl.ds(at, tile)
            taps = [
                lambda lanes, t=t: ahead[
                    pl.ds(pl.multiple_of(at + (KW - 1 - t) * run, run), tile), lanes
                ]
                for t in range(KW)
            ]
            grad_normed = taps_product(taps, kernels.at[layer])
            normed = padded[layer, pl.ds(pl.multiple_of(at + run, run), tile), :]
            value = stream_grad(layer, grad[rows, :], rows, normed, grad_normed)
            if bottom:
                high, low = split16(value)
                out16[rows, :] = high
                active_t[:, rows] = low.T
            else:
                grad[rows, :] = value
            return 0

        lax.fori_loop(0, tiles, stream_tile, 0)
        if not bottom:
            grad_normed = taps_product(
                [lambda lanes, v=v: v[:, lanes] for v in reversed(windows)], kernels.at[layer]
            )
            normed = padded[layer, count + 2 * run :, :]
            rows = slice(count, count + HALO)
            grad[rows, :] = stream_grad(layer, grad[rows, :], rows, normed, grad_normed)

    arriving[-1][0].wait()
    value = lax.dot_general(
        feats[:count, :], out16[...], (((0,), (0,)), ((), ())), preferred_element_type=F32
    )
    rest = jnp.dot(active_t[...], feats[:count, :], preferred_element_type=F32)
    put(stem_at, value + rest.T)
    leave(stem_at, 2 * half_rows - stem_at)
    for copy in leaving:
        copy.wait()


def network_back(scalars, sums, saved, bounds, head_t, kernels_t, mix_t, half_rows):
    preacts, scales, padded, feats = saved
    layers, rows, channels = preacts.shape
    count = rows - HALO
    tiles = count // min(TILE, count)
    devices = len(sums)
    vmem = pl.BlockSpec(memory_space=pltpu.VMEM)
    hbm = pl.BlockSpec(memory_space=pl.ANY)
    return pl.pallas_call(
        functools.partial(backward_kernel, count // 32, devices, lax.axis_size("dp")),
        out_shape=[jax.ShapeDtypeStruct((half_rows, channels), F32)] * 2,
        in_specs=[pl.BlockSpec(memory_space=pltpu.SMEM)]
        + [vmem] * devices
        + [hbm] * 4
        + [vmem] * 2
        + [hbm] * 2,
        out_specs=[hbm] * 2,
        scratch_shapes=[pltpu.VMEM(x.shape, x.dtype) for x in saved]
        + [
            pltpu.VMEM(kernels_t.shape, BF16),
            pltpu.VMEM(mix_t.shape, BF16),
            pltpu.VMEM((2 * half_rows, channels), F32),
            pltpu.VMEM((rows, channels), F32),
            pltpu.VMEM(padded.shape[1:], BF16),
            pltpu.VMEM((channels, count), BF16),
            pltpu.VMEM((count, channels), BF16),
            pltpu.SemaphoreType.DMA((layers * (tiles + 5) + 1,)),
            pltpu.SemaphoreType.DMA((layers + 1,)),
        ],
        compiler_params=pltpu.CompilerParams(vmem_limit_bytes=60 * 1024 * 1024),
        name="network_back",
    )(scalars, *sums, *saved, bounds, head_t, kernels_t, mix_t)


def weights_kernel(conv_ref, mix_ref, kernels_ref, turned_ref, mix_t_ref):
    row = lax.broadcasted_iota(jnp.int32, (HALF_MXU, HALF_MXU), 0) // GROUP_WIDTH
    col = lax.broadcasted_iota(jnp.int32, (HALF_MXU, HALF_MXU), 1) // GROUP_WIDTH
    for tap in range(KW):
        for half in range(kernels_ref.shape[0]):
            taps = conv_ref[tap, :, half * HALF_MXU : (half + 1) * HALF_MXU].astype(F32)
            dense = jnp.concatenate([taps] * (HALF_MXU // GROUP_WIDTH), axis=0)
            dense = jnp.where(row == col, dense, 0.0)
            kernels_ref[half, tap] = dense.astype(BF16)
            turned_ref[half, tap] = dense.T.astype(BF16)
    mix_t_ref[...] = mix_ref[...].astype(F32).T.astype(BF16)


def dense_weights(conv_weight, mix_weight):
    layers, taps, width, channels = conv_weight.shape
    dense = (layers, channels // HALF_MXU, taps, HALF_MXU, HALF_MXU)
    by_layer = lambda shape: pl.BlockSpec(
        (None,) + shape[1:], lambda i: (i,) + (0,) * (len(shape) - 1)
    )
    return pl.pallas_call(
        weights_kernel,
        out_shape=[
            jax.ShapeDtypeStruct(dense, BF16),
            jax.ShapeDtypeStruct(dense, BF16),
            jax.ShapeDtypeStruct(mix_weight.shape, BF16),
        ],
        grid=(layers,),
        in_specs=[by_layer(conv_weight.shape), by_layer(mix_weight.shape)],
        out_specs=[by_layer(dense), by_layer(dense), by_layer(mix_weight.shape)],
        compiler_params=pltpu.CompilerParams(vmem_limit_bytes=32 * 1024 * 1024),
        cost_estimate=pl.CostEstimate(flops=0, bytes_accessed=2**24, transcendentals=0),
        name="dense_weights",
    )(conv_weight, mix_weight)


def swap(x, axis, step):
    return lax.ppermute(x, axis, [(i, i ^ step) for i in range(lax.axis_size(axis))])


def encode(values, out_ref):
    rows = values.shape[0]
    top = jnp.maximum(jnp.max(jnp.abs(values), axis=1, keepdims=True), 1e-30)
    exponent = jnp.ceil(jnp.log(top) * (1.0 / np.log(2.0)) + 1e-4)
    scale = jnp.exp(-exponent * np.log(2.0).astype(np.float32)) * 32767.0
    out_ref[:rows, :] = jnp.round(values * scale).astype(jnp.int32).astype(jnp.int16)
    out_ref[rows:, :] = jnp.zeros((HALO, values.shape[1]), jnp.int16)
    across = jnp.broadcast_to(exponent, (rows, LANES)).T[:HALO, :]
    out_ref[rows:, :rows] = across.astype(jnp.int32).astype(jnp.int16)


def decode(ref):
    rows = ref.shape[0] - HALO
    across = ref[rows:, :rows].astype(jnp.int32).astype(F32)
    exponent = jnp.concatenate([across] * (LANES // HALO), axis=0).T[:, :1]
    scale = jnp.exp(exponent * np.log(2.0).astype(np.float32)) * (1.0 / 32767.0)
    return ref[:rows, :].astype(jnp.int32).astype(F32) * scale


def cut_kernel(size, place_ref, *refs):
    inputs, outs = refs[:-size], refs[-size:]
    rows = inputs[0].shape[0] // size
    for k in range(size):
        at = pl.multiple_of((place_ref[0] ^ k) * rows, rows)
        value = inputs[0][pl.ds(at, rows), :]
        for ref in inputs[1:]:
            value = value + ref[pl.ds(at, rows), :]
        if k:
            encode(value, outs[k])
        else:
            outs[0][...] = value


def sum_kernel(first_ref, *refs):
    value = first_ref[...]
    for ref in refs[:-1]:
        value = value + decode(ref)
    refs[-1][...] = value


def pieces_kernel(place_ref, *refs):
    inputs, out_ref = refs[:-1], refs[-1]
    rows = inputs[0].shape[0] - HALO
    for k, ref in enumerate(inputs):
        at = pl.multiple_of((place_ref[0] ^ k) * rows, rows)
        out_ref[pl.ds(at, rows), :] = decode(ref)


def encode_kernel(x_ref, out_ref):
    encode(x_ref[...], out_ref)


def small_call(kernel, name, out_shape, place, *args):
    vmem = pl.BlockSpec(memory_space=pltpu.VMEM)
    smem = pl.BlockSpec(memory_space=pltpu.SMEM)
    several = isinstance(out_shape, list)
    lead = [] if place is None else [place.reshape(1).astype(jnp.int32)]
    return pl.pallas_call(
        kernel,
        out_shape=out_shape,
        in_specs=[smem] * len(lead) + [vmem] * len(args),
        out_specs=[vmem] * len(out_shape) if several else vmem,
        compiler_params=pltpu.CompilerParams(vmem_limit_bytes=32 * 1024 * 1024),
        name=name,
    )(*lead, *args)


def scatter_pieces(parts, coded, axis, stride):
    size = lax.axis_size(axis) // stride
    place = lax.axis_index(axis) // stride
    rows, channels = parts[0].shape[0] // size, parts[0].shape[1]
    if coded:
        whole = jax.ShapeDtypeStruct(parts[0].shape, F32)
        parts = [small_call(sum_kernel, "sum_pieces", whole, None, *parts)]
    shapes = [jax.ShapeDtypeStruct((rows, channels), F32)]
    shapes += [jax.ShapeDtypeStruct((rows + HALO, channels), jnp.int16)] * (size - 1)
    own, *others = small_call(
        functools.partial(cut_kernel, size), "cut_pieces", shapes, place, *parts
    )
    return [own] + [swap(piece, axis, (k + 1) * stride) for k, piece in enumerate(others)]


def gather_pieces(x, axis, stride):
    size = lax.axis_size(axis) // stride
    place = lax.axis_index(axis) // stride
    rows, channels = x.shape
    shape = jax.ShapeDtypeStruct((rows + HALO, channels), jnp.int16)
    coded = small_call(encode_kernel, "code_piece", shape, None, x)
    pieces = [coded] + [swap(coded, axis, k * stride) for k in range(1, size)]
    whole = jax.ShapeDtypeStruct((size * rows, channels), F32)
    return small_call(pieces_kernel, "lay_pieces", whole, place, *pieces)


def spread_half(core, half_ref, is_mine, outs, sems):
    half_rows = half_ref.shape[0]
    for half in range(2):

        @pl.when((core == half) if is_mine else (core != half))
        def _(half=half):
            copies, first = [], 0
            for out_ref in outs:
                low = max(first, half * half_rows)
                high = min(first + out_ref.shape[0], (half + 1) * half_rows)
                if low < high:
                    copies.append(
                        pltpu.make_async_copy(
                            half_ref.at[pl.ds(low - half * half_rows, high - low), :],
                            out_ref.at[pl.ds(low - first, high - low), :],
                            sems.at[len(copies)],
                        )
                    )
                first += out_ref.shape[0]
            for copy in copies:
                copy.start()
            for copy in copies:
                copy.wait()


def spread_mine(core_ref, mine_ref, *refs):
    spread_half(core_ref[0], mine_ref, True, refs[:-1], refs[-1])


def spread_other(classes, head_at, core_ref, mine_ref, other_ref, *refs):
    refs = refs[(len(refs) - 3) // 2 :]
    *outs, head_ref, loss_ref, sems = refs
    spread_half(core_ref[0], other_ref, False, outs, sems)
    half, at = divmod(head_at, mine_ref.shape[0])
    mine, other = mine_ref[at : at + HALO, :], other_ref[at : at + HALO, :]
    ends = jnp.where(core_ref[0] == half, mine, other)
    head_ref[...] = ends[:classes]
    loss_ref[...] = ends[HALO - 1 : HALO, :1]


def sum_everywhere(kept, sent, sizes, classes):
    core = (lax.axis_index("dp") % 2).reshape(1).astype(jnp.int32)
    parts = scatter_pieces([kept, swap(sent, "dp", 1)], False, "dp", 2)
    parts = scatter_pieces(parts, True, "freq", 1)
    x = small_call(
        sum_kernel, "sum_pieces", jax.ShapeDtypeStruct(parts[0].shape, F32), None, *parts
    )
    x = gather_pieces(x, "freq", 1)
    x = gather_pieces(x, "dp", 2)
    other = swap(x, "dp", 1)
    channels = x.shape[1]
    shapes = [jax.ShapeDtypeStruct((rows, channels), F32) for rows in sizes[:-1]]
    hbm = pl.BlockSpec(memory_space=pl.ANY)
    vmem = pl.BlockSpec(memory_space=pltpu.VMEM)
    smem = pl.BlockSpec(memory_space=pltpu.SMEM)
    sems = [pltpu.SemaphoreType.DMA((len(sizes),))]
    halves = pl.pallas_call(
        spread_mine,
        out_shape=shapes,
        in_specs=[smem, vmem],
        out_specs=[hbm] * len(shapes),
        scratch_shapes=sems,
        cost_estimate=pl.CostEstimate(flops=0, bytes_accessed=2**23, transcendentals=0),
        name="spread_mine",
    )(core, x)
    return pl.pallas_call(
        functools.partial(spread_other, classes, sum(sizes[:-1])),
        out_shape=shapes
        + [
            jax.ShapeDtypeStruct((classes, channels), F32),
            jax.ShapeDtypeStruct((1, 1), F32),
        ],
        in_specs=[smem, vmem, vmem] + [hbm] * len(shapes),
        out_specs=[hbm] * len(shapes) + [vmem] * 2,
        scratch_shapes=sems,
        input_output_aliases={3 + k: k for k in range(len(shapes))},
        name="spread_other",
    )(core, x, other, *halves)


def shifted(pieces, axis):
    size = len(pieces)
    return [pieces[0]] + [
        lax.ppermute(pieces[k], axis, [(i, (i + k) % size) for i in range(size)])
        for k in range(1, size)
    ]


def all_of(x, axis):
    size = lax.axis_size(axis)
    pieces = [x]
    for shift in range(1, size):
        pieces.append(lax.ppermute(x, axis, [(i, (i + shift) % size) for i in range(size)]))
    return pieces


def local(records, stem_weight, conv_weight, mix_weight, head_weight, labels, band_bounds):
    freq = lax.axis_size("freq")
    place = lax.axis_index("freq").astype(jnp.int32)
    first_len, cols = records.shape[2:]
    second_len = cols * freq
    total_len = first_len * second_len
    layers, channels = mix_weight.shape[:2]
    classes = head_weight.shape[1]
    blocks = first_len // 2 // LANES
    run = second_len // 8 // freq
    count = 32 * run

    section, twiddle = (jnp.asarray(t) for t in first_tables(first_len, second_len))
    spread, table, flip = (jnp.asarray(t) for t in second_tables(second_len))
    here = place.reshape(1)
    signals = freq // blocks
    chunks = 2 // signals
    sent = [
        first_section(here, records[0], c, signals, freq, section, twiddle) for c in range(chunks)
    ]
    arrived = [shifted(pieces, "freq") for pieces in sent]
    features = [
        second_section(here, a, second_len, total_len, spread, table, flip) for a in arrived
    ]
    received = [piece for f in features for piece in shifted(f, "freq")]
    kernels, kernels_t, mix_t = dense_weights(conv_weight, mix_weight)
    head_t = jnp.pad(head_weight.T, ((0, HALO - classes), (0, 0)))
    steps = jnp.repeat(band_bounds // POOL, GROUP_WIDTH)
    bounds = jnp.stack([steps[:channels], steps[GROUP_WIDTH:]]).astype(jnp.int32)

    vmem = pl.BlockSpec(memory_space=pltpu.VMEM)
    hbm = pl.BlockSpec(memory_space=pl.ANY)
    smem = pl.BlockSpec(memory_space=pltpu.SMEM)
    saved = [
        ((layers, count + HALO, channels), F32),
        ((layers, count + HALO, LANES), F32),
        ((layers, count + 2 * run + HALO, channels), BF16),
        ((count + HALO, 2 * LANES), BF16),
    ]
    *kept, partial = pl.pallas_call(
        functools.partial(forward_kernel, run, freq, chunks),
        out_shape=[jax.ShapeDtypeStruct(s, d) for s, d in saved]
        + [jax.ShapeDtypeStruct((8, channels), F32)],
        in_specs=[smem] + [vmem] * len(received) + [hbm] * 3 + [vmem],
        out_specs=[hbm] * 4 + [vmem],
        scratch_shapes=[pltpu.VMEM(s, d) for s, d in saved]
        + [
            pltpu.VMEM(stem_weight.shape, BF16),
            pltpu.VMEM(kernels.shape, BF16),
            pltpu.VMEM(mix_weight.shape, BF16),
            pltpu.VMEM((count + HALO, channels), F32),
            pltpu.VMEM((HALO, channels), F32),
            pltpu.SemaphoreType.DMA((3 * layers + 1,)),
            pltpu.SemaphoreType.DMA((2 * layers + 1,)),
            pltpu.SemaphoreType.DMA((layers, count // min(TILE, count))),
        ],
        compiler_params=pltpu.CompilerParams(vmem_limit_bytes=56 * 1024 * 1024),
        name="network_ahead",
    )(here, *received, stem_weight, kernels, mix_weight, bounds)

    sums = all_of(partial, "freq")
    core = (lax.axis_index("dp") % 2).astype(jnp.int32)
    scalars = jnp.stack([place, labels[0], jnp.int32(classes), core])
    sizes = [layers * channels, 2 * LANES, layers * KW * GROUP_WIDTH, HALO]
    step = HALO * lax.axis_size("dp") // 2 * freq
    half_rows = -(-sum(sizes) // (2 * step)) * step
    halves = network_back(scalars, sums, kept, bounds, head_t, kernels_t, mix_t, half_rows)
    mix, stem, conv, head, loss = sum_everywhere(*halves, sizes, classes)
    return (
        loss.reshape(()),
        stem,
        conv.reshape(layers, KW, GROUP_WIDTH, channels),
        mix.reshape(layers, channels, channels),
        head.T,
    )


def solution(mesh):
    in_specs = (P("dp", None, None, "freq"), P(), P(), P(), P(), P("dp"), P())
    out_specs = (P(), P(), P(), P(), P())
    return jax.shard_map(local, mesh=mesh, in_specs=in_specs, out_specs=out_specs, check_vma=False)
```

profile of v0, /device:TPU:0, one launch (start us, length us, event | category | flops | bytes accessed | tf_op | source)
XLA Modules:
  0.0 222.4 jit_solution(9115914870274155104)
XLA Ops:
  0.6 8.7 %first_section.3 = (s16[528,256]{1,0:T(8,128)(2,1)}, s16[528,256]{1,0:T(8,128)(2,1)}, s16[528,256]{1,0:T(8,128)(2,1)}, s16[528,256]{1,0:T(8,128)(2,1)}) custom-call(s32[1]{0:T(128)} %bitcast.2.place_ref, f32[2,1024,512]{2,1,0:T(8,128)} %bitcast.9, bf16[2,1024,1024]{2,1,0:T(8,128)(2,1)} %constant.76.clone.table_ref, f32[2048,1024]{1,0:T(8,128)} %constant.77.clone.twiddle_ref), custom_call_target="tpu_custom_call" | custom-call | flops 3221225472 | bytes 8388608 | tf_op jit(solution)/shard_map/first_section/pallas_call | solution.py:107
  9.3 3.0 %collective-permute-start.6 = (s16[528,256]{1,0:T(8,128)(2,1)}, s16[528,256]{1,0:T(8,128)(2,1)S(1)}, u32[]{:S(2)}, u32[]{:S(2)}) collective-permute-start(s16[528,256]{1,0:T(8,128)(2,1)} %get-tuple-element.56), channel_id=1, source_target_pairs={{0,1},{1,2},{2,3},{3,0},{4,5},{5,6},{6,7},{7,4},{8,9},{9,10},{10,1... | collective-permute-start | bytes 811016 | tf_op jit(solution)/shard_map/ppermute | solution.py:854
  12.3 2.6 %collective-permute-start.7 = (s16[528,256]{1,0:T(8,128)(2,1)}, s16[528,256]{1,0:T(8,128)(2,1)S(1)}, u32[]{:S(2)}, u32[]{:S(2)}) collective-permute-start(s16[528,256]{1,0:T(8,128)(2,1)} %get-tuple-element.57), channel_id=1, source_target_pairs={{0,2},{1,3},{2,0},{3,1},{4,6},{5,7},{6,4},{7,5},{8,10},{9,11},{10,... | collective-permute-start | bytes 811016 | tf_op jit(solution)/shard_map/ppermute | solution.py:854
  16.3 8.6 %first_section.2 = (s16[528,256]{1,0:T(8,128)(2,1)}, s16[528,256]{1,0:T(8,128)(2,1)}, s16[528,256]{1,0:T(8,128)(2,1)}, s16[528,256]{1,0:T(8,128)(2,1)}) custom-call(s32[1]{0:T(128)} %bitcast.2.place_ref, f32[2,1024,512]{2,1,0:T(8,128)} %bitcast.10, bf16[2,1024,1024]{2,1,0:T(8,128)(2,1)} %constant.76.clone.table_ref, f32[2048,1024]{1,0:T(8,128)} %constant.77.clone.twiddle_ref), custom_call_target="tpu_custom_call" | custom-call | flops 3221225472 | bytes 8388608 | tf_op jit(solution)/shard_map/first_section/pallas_call | solution.py:107
  26.0 2.9 %collective-permute-start.2 = (s16[528,256]{1,0:T(8,128)(2,1)}, s16[528,256]{1,0:T(8,128)(2,1)S(1)}, u32[]{:S(2)}, u32[]{:S(2)}) collective-permute-start(s16[528,256]{1,0:T(8,128)(2,1)} %get-tuple-element.50), channel_id=1, source_target_pairs={{0,3},{1,0},{2,1},{3,2},{4,7},{5,4},{6,5},{7,6},{8,11},{9,8},{10,9... | collective-permute-start | bytes 811016 | tf_op jit(solution)/shard_map/ppermute | solution.py:854
  28.8 4.8 %collective-permute-done.7.refs_2_ = s16[528,256]{1,0:T(8,128)(2,1)S(1)} collective-permute-done((s16[528,256]{1,0:T(8,128)(2,1)}, s16[528,256]{1,0:T(8,128)(2,1)S(1)}, u32[]{:S(2)}, u32[]{:S(2)}) %collective-permute-start.7) | collective-permute-done | bytes 270368 | tf_op jit(solution)/shard_map/ppermute | solution.py:854
  33.7 1.6 copy-done.11
  36.7 8.2 %second_section.3 = (bf16[528,128]{1,0:T(8,128)(2,1)S(1)}, bf16[528,128]{1,0:T(8,128)(2,1)S(1)}, bf16[528,128]{1,0:T(8,128)(2,1)S(1)}, bf16[528,128]{1,0:T(8,128)(2,1)S(1)}) custom-call(s32[1]{0:T(128)} %bitcast.2.place_ref, s16[528,256]{1,0:T(8,128)(2,1)S(1)} %copy-done.10, s16[528,256]{1,0:T(8,128)(2,1)S(1)} %collective-permute-done.6.refs_1_, ...), custom_call_target="tpu_custom_call" | custom-call | flops 3221225472 | bytes 8388608 | tf_op jit(solution)/shard_map/second_section/pallas_call | solution.py:212
  45.6 17.1 %collective-permute-start.9 = (bf16[528,128]{1,0:T(8,128)(2,1)S(1)}, bf16[528,128]{1,0:T(8,128)(2,1)S(1)}, u32[]{:S(2)}, u32[]{:S(2)}) collective-permute-start(bf16[528,128]{1,0:T(8,128)(2,1)S(1)} %get-tuple-element.60), channel_id=1, source_target_pairs={{0,1},{1,2},{2,3},{3,0},{4,5},{5,6},{6,7},{7,4},{8,9},{9,10},{10,1... | collective-permute-start | bytes 405512 | tf_op jit(solution)/shard_map/ppermute | solution.py:854
  62.6 2.7 %collective-permute-start.10 = (bf16[528,128]{1,0:T(8,128)(2,1)S(1)}, bf16[528,128]{1,0:T(8,128)(2,1)S(1)}, u32[]{:S(2)}, u32[]{:S(2)}) collective-permute-start(bf16[528,128]{1,0:T(8,128)(2,1)S(1)} %get-tuple-element.61), channel_id=1, source_target_pairs={{0,2},{1,3},{2,0},{3,1},{4,6},{5,7},{6,4},{7,5},{8,10},{9,11},{10,... | collective-permute-start | bytes 405512 | tf_op jit(solution)/shard_map/ppermute | solution.py:854
  65.6 8.2 %second_section.2 = (bf16[528,128]{1,0:T(8,128)(2,1)S(1)}, bf16[528,128]{1,0:T(8,128)(2,1)S(1)}, bf16[528,128]{1,0:T(8,128)(2,1)S(1)}, bf16[528,128]{1,0:T(8,128)(2,1)S(1)}) custom-call(s32[1]{0:T(128)} %bitcast.2.place_ref, s16[528,256]{1,0:T(8,128)(2,1)S(1)} %copy-done.9, s16[528,256]{1,0:T(8,128)(2,1)S(1)} %collective-permute-done.refs_1_, ...), custom_call_target="tpu_custom_call" | custom-call | flops 3221225472 | bytes 8388608 | tf_op jit(solution)/shard_map/second_section/pallas_call | solution.py:212
  74.5 2.0 collective-permute-start.3
  76.8 2.1 collective-permute-start.5
  87.5 17.4 %network_ahead.1 = (f32[3,2064,512]{2,1,0:T(8,128)}, f32[3,2064,128]{2,1,0:T(8,128)}, bf16[3,2192,512]{2,1,0:T(8,128)(2,1)}, bf16[2064,256]{1,0:T(8,128)(2,1)}, f32[8,512]{1,0:T(8,128)}) custom-call(s32[1]{0:T(128)} %bitcast.2.place_ref, bf16[528,128]{1,0:T(8,128)(2,1)} %copy-done.8, bf16[528,128]{1,0:T(8,128)(2,1)} %copy-done.18, ...), custom_call_target="tpu_custom_call" | custom-call | tf_op jit(solution)/shard_map/network_ahead/pallas_call | solution.py:906
  104.8 3.4 %collective-permute-start.14 = (f32[8,512]{1,0:T(8,128)}, f32[8,512]{1,0:T(8,128)S(1)}, u32[]{:S(2)}, u32[]{:S(2)}) collective-permute-start(f32[8,512]{1,0:T(8,128)} %get-tuple-element.64.refs_0_), channel_id=1, source_target_pairs={{0,3},{1,0},{2,1},{3,2},{4,7},{5,4},{6,5},{7,6},{8,11},{9,8},{10,9... | collective-permute-start | bytes 49160 | tf_op jit(solution)/shard_map/ppermute | solution.py:863
  108.7 11.4 %collective-permute-start.12 = (f32[8,512]{1,0:T(8,128)}, f32[8,512]{1,0:T(8,128)S(1)}, u32[]{:S(2)}, u32[]{:S(2)}) collective-permute-start(f32[8,512]{1,0:T(8,128)} %get-tuple-element.64.refs_0_), channel_id=1, source_target_pairs={{0,1},{1,2},{2,3},{3,0},{4,5},{5,6},{6,7},{7,4},{8,9},{9,10},{10,1... | collective-permute-start | bytes 49160 | tf_op jit(solution)/shard_map/ppermute | solution.py:863
  121.3 4.4 %collective-permute-done.12.refs_1_ = f32[8,512]{1,0:T(8,128)S(1)} collective-permute-done((f32[8,512]{1,0:T(8,128)}, f32[8,512]{1,0:T(8,128)S(1)}, u32[]{:S(2)}, u32[]{:S(2)}) %collective-permute-start.12) | collective-permute-done | bytes 16416 | tf_op jit(solution)/shard_map/ppermute | solution.py:863
  126.3 31.3 %network_back.1 = (f32[1024,512]{1,0:T(8,128)}, f32[1024,512]{1,0:T(8,128)}) custom-call(s32[4]{0:T(128)} %pad_add_fusion.1.place_ref, f32[8,512]{1,0:T(8,128)} %get-tuple-element.64.refs_0_, f32[8,512]{1,0:T(8,128)} %copy-done.24, f32[8,512]{1,0:T(8,128)} %copy-done.23, f32[8,512]{1,0:T(8,128)} %copy-done.22, f32[3,2064,512]{2,1,0:T(8,128)} %get-tuple-element.65.refs_4_, ...), custom_call_target="tpu_custom_call" | custom-call | tf_op jit(solution)/shard_map/network_back/pallas_call | solution.py:613
  157.6 4.3 %collective-permute-done.15.refs_1_ = f32[1024,512]{1,0:T(8,128)S(1)} collective-permute-done((f32[1024,512]{1,0:T(8,128)}, f32[1024,512]{1,0:T(8,128)S(1)}, u32[]{:S(2)}, u32[]{:S(2)}) %collective-permute-start.15) | collective-permute-done | bytes 2097184 | tf_op jit(solution)/shard_map/ppermute | solution.py:675
  162.0 1.6 copy-done.4
  167.6 6.0 %collective-permute-done.16.refs_0_ = s16[272,512]{1,0:T(8,128)(2,1)S(1)} collective-permute-done((s16[272,512]{1,0:T(8,128)(2,1)S(1)}, s16[272,512]{1,0:T(8,128)(2,1)S(1)}, u32[]{:S(2)}, u32[]{:S(2)}) %collective-permute-start.16) | collective-permute-done | bytes 278560 | tf_op jit(solution)/shard_map/ppermute | solution.py:675
  173.6 6.4 %collective-permute-done.17.refs_1_ = s16[272,512]{1,0:T(8,128)(2,1)S(1)} collective-permute-done((s16[272,512]{1,0:T(8,128)(2,1)S(1)}, s16[272,512]{1,0:T(8,128)(2,1)S(1)}, u32[]{:S(2)}, u32[]{:S(2)}) %collective-permute-start.17) | collective-permute-done | bytes 278560 | tf_op jit(solution)/shard_map/ppermute | solution.py:675
  181.3 3.7 %collective-permute-start.21 = (s16[80,512]{1,0:T(8,128)(2,1)S(1)}, s16[80,512]{1,0:T(8,128)(2,1)S(1)}, u32[]{:S(2)}, u32[]{:S(2)}) collective-permute-start(s16[80,512]{1,0:T(8,128)(2,1)S(1)} %get-tuple-element.80), channel_id=1, source_target_pairs={{0,3},{1,2},{2,1},{3,0},{4,7},{5,6},{6,5},{7,4},{8,11},{9,10},{10,... | collective-permute-start | bytes 245768 | tf_op jit(solution)/shard_map/ppermute | solution.py:675
  185.1 4.4 %collective-permute-done.20.refs_1_ = s16[80,512]{1,0:T(8,128)(2,1)S(1)} collective-permute-done((s16[80,512]{1,0:T(8,128)(2,1)S(1)}, s16[80,512]{1,0:T(8,128)(2,1)S(1)}, u32[]{:S(2)}, u32[]{:S(2)}) %collective-permute-start.20) | collective-permute-done | bytes 81952 | tf_op jit(solution)/shard_map/ppermute | solution.py:675
  189.8 1.9 collective-permute-start.24
  194.2 2.0 collective-permute-done.24.refs_3_
  196.2 2.4 %collective-permute-done.23.refs_2_ = s16[80,512]{1,0:T(8,128)(2,1)S(1)} collective-permute-done((s16[80,512]{1,0:T(8,128)(2,1)S(1)}, s16[80,512]{1,0:T(8,128)(2,1)S(1)}, u32[]{:S(2)}, u32[]{:S(2)}) %collective-permute-start.23) | collective-permute-done | bytes 81952 | tf_op jit(solution)/shard_map/ppermute | solution.py:675
  200.2 1.8 collective-permute-start.26
  202.6 7.0 %collective-permute-done.27.refs_3_ = s16[272,512]{1,0:T(8,128)(2,1)S(1)} collective-permute-done((s16[272,512]{1,0:T(8,128)(2,1)S(1)}, s16[272,512]{1,0:T(8,128)(2,1)S(1)}, u32[]{:S(2)}, u32[]{:S(2)}) %collective-permute-start.27) | collective-permute-done | bytes 278560 | tf_op jit(solution)/shard_map/ppermute | solution.py:675
  209.6 3.6 %collective-permute-done.26.refs_2_ = s16[272,512]{1,0:T(8,128)(2,1)S(1)} collective-permute-done((s16[272,512]{1,0:T(8,128)(2,1)S(1)}, s16[272,512]{1,0:T(8,128)(2,1)S(1)}, u32[]{:S(2)}, u32[]{:S(2)}) %collective-permute-start.26) | collective-permute-done | bytes 278560 | tf_op jit(solution)/shard_map/ppermute | solution.py:675
  215.0 2.9 %spread_mine.1 = (f32[1536,512]{1,0:T(8,128)}, f32[256,512]{1,0:T(8,128)}, f32[144,512]{1,0:T(8,128)}) custom-call(s32[1]{0:T(128)} %bitcast.core_ref, f32[1024,512]{1,0:T(8,128)} %copy-done), custom_call_target="tpu_custom_call" | custom-call | bytes 8388608 | tf_op jit(solution)/shard_map/spread_mine/pallas_call | solution.py:827
  218.0 4.1 %spread_other.1 = (f32[1536,512]{1,0:T(8,128)}, f32[256,512]{1,0:T(8,128)}, f32[144,512]{1,0:T(8,128)}, f32[10,512]{1,0:T(8,128)}, f32[1,1]{1,0:T(1,128)}) custom-call(s32[1]{0:T(128)} %bitcast.core_ref, f32[1024,512]{1,0:T(8,128)} %copy-done, ...), custom_call_target="tpu_custom_call", output_to_operand_aliasing={{0}: (3, {}), {1}: (4, {}), {2}: (5, {})} | custom-call | tf_op jit(solution)/shard_map/spread_other/pallas_call | solution.py:836
  (104 shorter events, 28.2 us)
Async XLA Ops:
  9.3 16.6 %collective-permute-start.6 = (s16[528,256]{1,0:T(8,128)(2,1)}, s16[528,256]{1,0:T(8,128)(2,1)S(1)}, u32[]{:S(2)}, u32[]{:S(2)}) collective-permute-start(s16[528,256]{1,0:T(8,128)(2,1)} %get-tuple-element.56), channel_id=1, source_target_pairs={{0,1},{1,2},{2,3},{3,0},{4,5},{5,6},{6,7},{7,4},{8,9},{9,10},{10,1... | collective-permute-start | bytes 811016 | tf_op jit(solution)/shard_map/ppermute | solution.py:854
  12.3 21.3 %collective-permute-start.7 = (s16[528,256]{1,0:T(8,128)(2,1)}, s16[528,256]{1,0:T(8,128)(2,1)S(1)}, u32[]{:S(2)}, u32[]{:S(2)}) collective-permute-start(s16[528,256]{1,0:T(8,128)(2,1)} %get-tuple-element.57), channel_id=1, source_target_pairs={{0,2},{1,3},{2,0},{3,1},{4,6},{5,7},{6,4},{7,5},{8,10},{9,11},{10,... | collective-permute-start | bytes 811016 | tf_op jit(solution)/shard_map/ppermute | solution.py:854
  14.9 18.7 %collective-permute-start.8 = (s16[528,256]{1,0:T(8,128)(2,1)}, s16[528,256]{1,0:T(8,128)(2,1)S(1)}, u32[]{:S(2)}, u32[]{:S(2)}) collective-permute-start(s16[528,256]{1,0:T(8,128)(2,1)} %get-tuple-element.58), channel_id=1, source_target_pairs={{0,3},{1,0},{2,1},{3,2},{4,7},{5,4},{6,5},{7,6},{8,11},{9,8},{10,9... | collective-permute-start | bytes 811016 | tf_op jit(solution)/shard_map/ppermute | solution.py:854
  24.9 40.4 %collective-permute-start = (s16[528,256]{1,0:T(8,128)(2,1)}, s16[528,256]{1,0:T(8,128)(2,1)S(1)}, u32[]{:S(2)}, u32[]{:S(2)}) collective-permute-start(s16[528,256]{1,0:T(8,128)(2,1)} %get-tuple-element.48), channel_id=1, source_target_pairs={{0,1},{1,2},{2,3},{3,0},{4,5},{5,6},{6,7},{7,4},{8,9},{9,10},{10,1... | collective-permute-start | bytes 811016 | tf_op jit(solution)/shard_map/ppermute | solution.py:854
  25.6 40.0 %collective-permute-start.1 = (s16[528,256]{1,0:T(8,128)(2,1)}, s16[528,256]{1,0:T(8,128)(2,1)S(1)}, u32[]{:S(2)}, u32[]{:S(2)}) collective-permute-start(s16[528,256]{1,0:T(8,128)(2,1)} %get-tuple-element.49), channel_id=1, source_target_pairs={{0,2},{1,3},{2,0},{3,1},{4,6},{5,7},{6,4},{7,5},{8,10},{9,11},{10,... | collective-permute-start | bytes 811016 | tf_op jit(solution)/shard_map/ppermute | solution.py:854
  26.0 39.6 %collective-permute-start.2 = (s16[528,256]{1,0:T(8,128)(2,1)}, s16[528,256]{1,0:T(8,128)(2,1)S(1)}, u32[]{:S(2)}, u32[]{:S(2)}) collective-permute-start(s16[528,256]{1,0:T(8,128)(2,1)} %get-tuple-element.50), channel_id=1, source_target_pairs={{0,3},{1,0},{2,1},{3,2},{4,7},{5,4},{6,5},{7,6},{8,11},{9,8},{10,9... | collective-permute-start | bytes 811016 | tf_op jit(solution)/shard_map/ppermute | solution.py:854
  36.7 28.9 %copy-start.9 = (s16[528,256]{1,0:T(8,128)(2,1)S(1)}, s16[528,256]{1,0:T(8,128)(2,1)}, u32[]{:S(2)}) copy-start(s16[528,256]{1,0:T(8,128)(2,1)} %get-tuple-element.47.refs_0_) | copy-start | bytes 811012
  36.7 28.9 %copy-start.12 = (bf16[2,512,1024]{2,1,0:T(8,128)(2,1)S(1)}, bf16[2,512,1024]{2,1,0:T(8,128)(2,1)}, u32[]{:S(2)}) copy-start(bf16[2,512,1024]{2,1,0:T(8,128)(2,1)} %constant.79.clone.refs_5_) | copy-start | bytes 6291460
  45.6 31.2 %collective-permute-start.9 = (bf16[528,128]{1,0:T(8,128)(2,1)S(1)}, bf16[528,128]{1,0:T(8,128)(2,1)S(1)}, u32[]{:S(2)}, u32[]{:S(2)}) collective-permute-start(bf16[528,128]{1,0:T(8,128)(2,1)S(1)} %get-tuple-element.60), channel_id=1, source_target_pairs={{0,1},{1,2},{2,3},{3,0},{4,5},{5,6},{6,7},{7,4},{8,9},{9,10},{10,1... | collective-permute-start | bytes 405512 | tf_op jit(solution)/shard_map/ppermute | solution.py:854
  62.6 23.3 %collective-permute-start.10 = (bf16[528,128]{1,0:T(8,128)(2,1)S(1)}, bf16[528,128]{1,0:T(8,128)(2,1)S(1)}, u32[]{:S(2)}, u32[]{:S(2)}) collective-permute-start(bf16[528,128]{1,0:T(8,128)(2,1)S(1)} %get-tuple-element.61), channel_id=1, source_target_pairs={{0,2},{1,3},{2,0},{3,1},{4,6},{5,7},{6,4},{7,5},{8,10},{9,11},{10,... | collective-permute-start | bytes 405512 | tf_op jit(solution)/shard_map/ppermute | solution.py:854
  65.3 20.6 %collective-permute-start.11 = (bf16[528,128]{1,0:T(8,128)(2,1)S(1)}, bf16[528,128]{1,0:T(8,128)(2,1)S(1)}, u32[]{:S(2)}, u32[]{:S(2)}) collective-permute-start(bf16[528,128]{1,0:T(8,128)(2,1)S(1)} %get-tuple-element.62), channel_id=1, source_target_pairs={{0,3},{1,0},{2,1},{3,2},{4,7},{5,4},{6,5},{7,6},{8,11},{9,8},{10,9... | collective-permute-start | bytes 405512 | tf_op jit(solution)/shard_map/ppermute | solution.py:854
  74.5 11.5 %collective-permute-start.3 = (bf16[528,128]{1,0:T(8,128)(2,1)S(1)}, bf16[528,128]{1,0:T(8,128)(2,1)S(1)}, u32[]{:S(2)}, u32[]{:S(2)}) collective-permute-start(bf16[528,128]{1,0:T(8,128)(2,1)S(1)} %get-tuple-element.52), channel_id=1, source_target_pairs={{0,1},{1,2},{2,3},{3,0},{4,5},{5,6},{6,7},{7,4},{8,9},{9,10},{10,1... | collective-permute-start | bytes 405512 | tf_op jit(solution)/shard_map/ppermute | solution.py:854
  76.5 10.3 %collective-permute-start.4 = (bf16[528,128]{1,0:T(8,128)(2,1)S(1)}, bf16[528,128]{1,0:T(8,128)(2,1)S(1)}, u32[]{:S(2)}, u32[]{:S(2)}) collective-permute-start(bf16[528,128]{1,0:T(8,128)(2,1)S(1)} %get-tuple-element.53), channel_id=1, source_target_pairs={{0,2},{1,3},{2,0},{3,1},{4,6},{5,7},{6,4},{7,5},{8,10},{9,11},{10,... | collective-permute-start | bytes 405512 | tf_op jit(solution)/shard_map/ppermute | solution.py:854
  76.8 10.0 %collective-permute-start.5 = (bf16[528,128]{1,0:T(8,128)(2,1)S(1)}, bf16[528,128]{1,0:T(8,128)(2,1)S(1)}, u32[]{:S(2)}, u32[]{:S(2)}) collective-permute-start(bf16[528,128]{1,0:T(8,128)(2,1)S(1)} %get-tuple-element.54), channel_id=1, source_target_pairs={{0,3},{1,0},{2,1},{3,2},{4,7},{5,4},{6,5},{7,6},{8,11},{9,8},{10,9... | collective-permute-start | bytes 405512 | tf_op jit(solution)/shard_map/ppermute | solution.py:854
  87.5 33.2 %copy-start.21 = (f32[512,10]{0,1:T(8,128)S(1)}, f32[512,10]{0,1:T(8,128)}, u32[]{:S(2)}) copy-start(f32[512,10]{0,1:T(8,128)} %param.16) | copy-start | bytes 61444
  104.8 16.4 %collective-permute-start.14 = (f32[8,512]{1,0:T(8,128)}, f32[8,512]{1,0:T(8,128)S(1)}, u32[]{:S(2)}, u32[]{:S(2)}) collective-permute-start(f32[8,512]{1,0:T(8,128)} %get-tuple-element.64.refs_0_), channel_id=1, source_target_pairs={{0,3},{1,0},{2,1},{3,2},{4,7},{5,4},{6,5},{7,6},{8,11},{9,8},{10,9... | collective-permute-start | bytes 49160 | tf_op jit(solution)/shard_map/ppermute | solution.py:863
  108.2 13.1 %collective-permute-start.13 = (f32[8,512]{1,0:T(8,128)}, f32[8,512]{1,0:T(8,128)S(1)}, u32[]{:S(2)}, u32[]{:S(2)}) collective-permute-start(f32[8,512]{1,0:T(8,128)} %get-tuple-element.64.refs_0_), channel_id=1, source_target_pairs={{0,2},{1,3},{2,0},{3,1},{4,6},{5,7},{6,4},{7,5},{8,10},{9,11},{10,... | collective-permute-start | bytes 49160 | tf_op jit(solution)/shard_map/ppermute | solution.py:863
  108.7 17.0 %collective-permute-start.12 = (f32[8,512]{1,0:T(8,128)}, f32[8,512]{1,0:T(8,128)S(1)}, u32[]{:S(2)}, u32[]{:S(2)}) collective-permute-start(f32[8,512]{1,0:T(8,128)} %get-tuple-element.64.refs_0_), channel_id=1, source_target_pairs={{0,1},{1,2},{2,3},{3,0},{4,5},{5,6},{6,7},{7,4},{8,9},{9,10},{10,1... | collective-permute-start | bytes 49160 | tf_op jit(solution)/shard_map/ppermute | solution.py:863
  157.6 4.4 %collective-permute-start.15 = (f32[1024,512]{1,0:T(8,128)}, f32[1024,512]{1,0:T(8,128)S(1)}, u32[]{:S(2)}, u32[]{:S(2)}) collective-permute-start(f32[1024,512]{1,0:T(8,128)} %get-tuple-element.72), channel_id=1, source_target_pairs={{0,4},{4,0},{8,12},{12,8},{16,20},{20,16},{24,28},{28,24},{1,5},{5... | collective-permute-start | bytes 6291464 | tf_op jit(solution)/shard_map/ppermute | solution.py:675
  164.1 9.5 %collective-permute-start.16 = (s16[272,512]{1,0:T(8,128)(2,1)S(1)}, s16[272,512]{1,0:T(8,128)(2,1)S(1)}, u32[]{:S(2)}, u32[]{:S(2)}) collective-permute-start(s16[272,512]{1,0:T(8,128)(2,1)S(1)} %get-tuple-element.74), channel_id=1, source_target_pairs={{0,8},{4,12},{8,0},{12,4},{16,24},{20,28},{24,16},{28,20},{1,9},{5... | collective-permute-start | bytes 835592 | tf_op jit(solution)/shard_map/ppermute | solution.py:675
  165.6 14.4 %collective-permute-start.17 = (s16[272,512]{1,0:T(8,128)(2,1)S(1)}, s16[272,512]{1,0:T(8,128)(2,1)S(1)}, u32[]{:S(2)}, u32[]{:S(2)}) collective-permute-start(s16[272,512]{1,0:T(8,128)(2,1)S(1)} %get-tuple-element.75), channel_id=1, source_target_pairs={{0,16},{4,20},{8,24},{12,28},{16,0},{20,4},{24,8},{28,12},{1,17},{... | collective-permute-start | bytes 835592 | tf_op jit(solution)/shard_map/ppermute | solution.py:675
  167.2 12.9 %collective-permute-start.18 = (s16[272,512]{1,0:T(8,128)(2,1)S(1)}, s16[272,512]{1,0:T(8,128)(2,1)S(1)}, u32[]{:S(2)}, u32[]{:S(2)}) collective-permute-start(s16[272,512]{1,0:T(8,128)(2,1)S(1)} %get-tuple-element.76), channel_id=1, source_target_pairs={{0,24},{4,28},{8,16},{12,20},{16,8},{20,12},{24,0},{28,4},{1,25},{... | collective-permute-start | bytes 835592 | tf_op jit(solution)/shard_map/ppermute | solution.py:675
  180.6 4.5 %collective-permute-start.19 = (s16[80,512]{1,0:T(8,128)(2,1)S(1)}, s16[80,512]{1,0:T(8,128)(2,1)S(1)}, u32[]{:S(2)}, u32[]{:S(2)}) collective-permute-start(s16[80,512]{1,0:T(8,128)(2,1)S(1)} %get-tuple-element.78), channel_id=1, source_target_pairs={{0,1},{1,0},{2,3},{3,2},{4,5},{5,4},{6,7},{7,6},{8,9},{9,8},{10,11... | collective-permute-start | bytes 245768 | tf_op jit(solution)/shard_map/ppermute | solution.py:675
  180.7 8.8 %collective-permute-start.20 = (s16[80,512]{1,0:T(8,128)(2,1)S(1)}, s16[80,512]{1,0:T(8,128)(2,1)S(1)}, u32[]{:S(2)}, u32[]{:S(2)}) collective-permute-start(s16[80,512]{1,0:T(8,128)(2,1)S(1)} %get-tuple-element.79), channel_id=1, source_target_pairs={{0,2},{1,3},{2,0},{3,1},{4,6},{5,7},{6,4},{7,5},{8,10},{9,11},{10,... | collective-permute-start | bytes 245768 | tf_op jit(solution)/shard_map/ppermute | solution.py:675
  181.3 8.1 %collective-permute-start.21 = (s16[80,512]{1,0:T(8,128)(2,1)S(1)}, s16[80,512]{1,0:T(8,128)(2,1)S(1)}, u32[]{:S(2)}, u32[]{:S(2)}) collective-permute-start(s16[80,512]{1,0:T(8,128)(2,1)S(1)} %get-tuple-element.80), channel_id=1, source_target_pairs={{0,3},{1,2},{2,1},{3,0},{4,7},{5,6},{6,5},{7,4},{8,11},{9,10},{10,... | collective-permute-start | bytes 245768 | tf_op jit(solution)/shard_map/ppermute | solution.py:675
  189.8 6.4 %collective-permute-start.24 = (s16[80,512]{1,0:T(8,128)(2,1)S(1)}, s16[80,512]{1,0:T(8,128)(2,1)S(1)}, u32[]{:S(2)}, u32[]{:S(2)}) collective-permute-start(s16[80,512]{1,0:T(8,128)(2,1)S(1)} %code_piece.2.refs_0_), channel_id=1, source_target_pairs={{0,3},{1,2},{2,1},{3,0},{4,7},{5,6},{6,5},{7,4},{8,11},{9,10},{10,... | collective-permute-start | bytes 245768 | tf_op jit(solution)/shard_map/ppermute | solution.py:675
  191.8 6.8 %collective-permute-start.23 = (s16[80,512]{1,0:T(8,128)(2,1)S(1)}, s16[80,512]{1,0:T(8,128)(2,1)S(1)}, u32[]{:S(2)}, u32[]{:S(2)}) collective-permute-start(s16[80,512]{1,0:T(8,128)(2,1)S(1)} %code_piece.2.refs_0_), channel_id=1, source_target_pairs={{0,2},{1,3},{2,0},{3,1},{4,6},{5,7},{6,4},{7,5},{8,10},{9,11},{10,... | collective-permute-start | bytes 245768 | tf_op jit(solution)/shard_map/ppermute | solution.py:675
  192.8 5.9 %collective-permute-start.22 = (s16[80,512]{1,0:T(8,128)(2,1)S(1)}, s16[80,512]{1,0:T(8,128)(2,1)S(1)}, u32[]{:S(2)}, u32[]{:S(2)}) collective-permute-start(s16[80,512]{1,0:T(8,128)(2,1)S(1)} %code_piece.2.refs_0_), channel_id=1, source_target_pairs={{0,1},{1,0},{2,3},{3,2},{4,5},{5,4},{6,7},{7,6},{8,9},{9,8},{10,11... | collective-permute-start | bytes 245768 | tf_op jit(solution)/shard_map/ppermute | solution.py:675
  199.0 10.6 %collective-permute-start.27 = (s16[272,512]{1,0:T(8,128)(2,1)S(1)}, s16[272,512]{1,0:T(8,128)(2,1)S(1)}, u32[]{:S(2)}, u32[]{:S(2)}) collective-permute-start(s16[272,512]{1,0:T(8,128)(2,1)S(1)} %code_piece.3.refs_0_), channel_id=1, source_target_pairs={{0,24},{4,28},{8,16},{12,20},{16,8},{20,12},{24,0},{28,4},{1,25},{... | collective-permute-start | bytes 835592 | tf_op jit(solution)/shard_map/ppermute | solution.py:675
  200.2 13.0 %collective-permute-start.26 = (s16[272,512]{1,0:T(8,128)(2,1)S(1)}, s16[272,512]{1,0:T(8,128)(2,1)S(1)}, u32[]{:S(2)}, u32[]{:S(2)}) collective-permute-start(s16[272,512]{1,0:T(8,128)(2,1)S(1)} %code_piece.3.refs_0_), channel_id=1, source_target_pairs={{0,16},{4,20},{8,24},{12,28},{16,0},{20,4},{24,8},{28,12},{1,17},{... | collective-permute-start | bytes 835592 | tf_op jit(solution)/shard_map/ppermute | solution.py:675
  202.0 11.3 %collective-permute-start.25 = (s16[272,512]{1,0:T(8,128)(2,1)S(1)}, s16[272,512]{1,0:T(8,128)(2,1)S(1)}, u32[]{:S(2)}, u32[]{:S(2)}) collective-permute-start(s16[272,512]{1,0:T(8,128)(2,1)S(1)} %code_piece.3.refs_0_), channel_id=1, source_target_pairs={{0,8},{4,12},{8,0},{12,4},{16,24},{20,28},{24,16},{28,20},{1,9},{5... | collective-permute-start | bytes 835592 | tf_op jit(solution)/shard_map/ppermute | solution.py:675
  213.7 4.4 %collective-permute-start.28 = (f32[1024,512]{1,0:T(8,128)S(1)}, f32[1024,512]{1,0:T(8,128)}, u32[]{:S(2)}, u32[]{:S(2)}) collective-permute-start(f32[1024,512]{1,0:T(8,128)S(1)} %lay_pieces.3.mine_ref), channel_id=1, source_target_pairs={{0,4},{4,0},{8,12},{12,8},{16,20},{20,16},{24,28},{28,24},{1,5},{5... | collective-permute-start | bytes 6291464 | tf_op jit(solution)/shard_map/ppermute | solution.py:675
  (23 other events, 111.7 us)
where the time goes:
time: 224 us; the launch traced here: 222 us
  Pallas kernels  93 us (42%)
  starting transfers between devices  66.5 us (30%)
  waiting for transfers between devices  46.3 us (21%)
  local copies, waits for them, and re-layouts  13.5 us (6%)
    ppermute x14, waiting for transfers between devices, swap(): lax.ppermute(x, axis, [(i, i ^ step) for i in range(lax.axis_size(axis))])  36.3 us
    ppermute x12, starting transfers between devices, shifted(): lax.ppermute(pieces[k], axis, [(i, (i + k) % size) for i in range(size)])  35.2 us
    pallas_call x1, Pallas kernels, network_back(): pl.pallas_call(functools.partial(backward_kernel, count // 32, devices, l...  31.3 us
    pallas_call x1, Pallas kernels, local(): pl.pallas_call(functools.partial(forward_kernel, run, freq, chunks), out_...  17.4 us
    pallas_call x2, Pallas kernels, first_section(): pl.pallas_call(functools.partial(first_kernel, devices), out_shape=[jax.S...  17.3 us
    pallas_call x2, Pallas kernels, second_section(): pl.pallas_call(functools.partial(second_kernel, devices, total_len), out_...  16.4 us
    ppermute x14, starting transfers between devices, swap(): lax.ppermute(x, axis, [(i, i ^ step) for i in range(lax.axis_size(axis))])  16.1 us
    ppermute x3, starting transfers between devices, all_of(): lax.ppermute(x, axis, [(i, (i + shift) % size) for i in range(size)])  15.2 us
  transfers between devices with their start and end apart: 29, of which 13 were waited for; matrix products, arithmetic and copies ran while one was open for 1% of the time, Pallas kernels for 13%

commit v1 on v0

--- a/solution.py
+++ b/solution.py
@@ -95,7 +95,7 @@
         codes[cols:, :] = head.astype(jnp.int32).astype(jnp.int16)
         for shift in range(devices):
 
-            @pl.when((place_ref[0] + shift) % devices == block * signals + signal)
+            @pl.when((place_ref[0] ^ shift) == block * signals + signal)
             def _(shift=shift):
                 outs[shift][...] = codes[...]
 
@@ -139,7 +139,7 @@
     quarter = signal.shape[0] // 4
     run = quarter // 2 // devices
     for shift in range(devices):
-        source = (place - shift + devices) % devices
+        source = place ^ shift
         head = received[shift][cols:, :].astype(jnp.int32).astype(F32)
         values = received[shift][:cols, :].astype(jnp.int32).astype(F32)
         rows = pl.ds(pl.multiple_of(source * cols, cols), cols)
@@ -200,7 +200,7 @@
     for to in range(devices):
         packed[to, 8 * run :, :] = edges[to].astype(BF16)
     for shift in range(devices):
-        outs[shift][...] = packed[(place + shift) % devices]
+        outs[shift][...] = packed[place ^ shift]
 
 
 def second_section(place, received, second_len, total_len, spread, table, flip):
@@ -296,7 +296,7 @@
     for chunk in range(chunks):
         for shift in range(devices):
             ref = received[chunk * devices + shift]
-            source = (place - shift + devices) % devices
+            source = place ^ shift
             ends = ref[8 * run :, :].astype(F32)
             channel = chunk if chunks == 2 else source % 2
             lanes = pl.ds(pl.multiple_of(channel * LANES, LANES), LANES)
@@ -407,7 +407,7 @@
 def backward_kernel(run, devices, all_records, place_ref, *refs):
     sums, refs = refs[:devices], refs[devices:]
     (preacts_in, scales_in, padded_in, feats_in, bounds, head, kernels_in, mix_in, kept, sent,
-     preacts, scales, padded, feats, kernels, mix_t, sums_out, grad, ahead, active_t, out16,
+     preacts, scales, padded, feats, kernels, mix_t, sums_out, codes, grad, ahead, active_t, out16,
      sems, sems_out) = refs
     layers = mix_t.shape[0]
     channels = grad.shape[1]
@@ -441,19 +441,24 @@
     def put(at, value):
         sums_out[at : at + value.shape[0], :] = value
 
-    def leave(at, rows):
-        half, to = divmod(at, half_rows)
-        source, sem = sums_out.at[pl.ds(at, rows), :], sems_out.at[len(leaving)]
-        to = pl.ds(to, rows)
-        leaving.append(pltpu.make_async_copy(source, kept.at[to, :], sem))
+    def leave(region):
+        half, inside = divmod(region, sent.shape[0])
+        rows = pl.ds(region * channels, channels)
+        sem = sems_out.at[region]
+        plain = pltpu.make_async_copy(
+            sums_out.at[rows, :], kept.at[pl.ds(inside * channels, channels), :], sem
+        )
+        coded = pltpu.make_async_copy(codes.at[region], sent.at[inside], sem)
+        leaving.append((half, plain, coded))
 
         @pl.when(core == half)
         def _():
-            pltpu.make_async_copy(source, kept.at[to, :], sem).start()
+            plain.start()
 
         @pl.when(core != half)
         def _():
-            pltpu.make_async_copy(source, sent.at[to, :], sem).start()
+            encode(sums_out[rows, :], codes.at[region])
+            coded.start()
 
     total = sums[0][...]
     for ref in sums[1:]:
@@ -540,7 +545,7 @@
             layer * channels,
             jnp.dot(active_t[...], out16[...], preferred_element_type=F32),
         )
-        leave(layer * channels, channels)
+        leave(layer)
 
         copies[tiles + 2].wait()
         for tap in range(KW):
@@ -597,9 +602,10 @@
     )
     rest = jnp.dot(active_t[...], feats[:count, :], preferred_element_type=F32)
     put(stem_at, value + rest.T)
-    leave(stem_at, 2 * half_rows - stem_at)
-    for copy in leaving:
-        copy.wait()
+    leave(layers)
+    for half, plain, coded in leaving:
+        pl.when(core == half)(plain.wait)
+        pl.when(core != half)(coded.wait)
 
 
 def network_back(scalars, sums, saved, bounds, head_t, kernels_t, mix_t, half_rows):
@@ -608,11 +614,15 @@
     count = rows - HALO
     tiles = count // min(TILE, count)
     devices = len(sums)
+    region = (channels + HALO, channels)
     vmem = pl.BlockSpec(memory_space=pltpu.VMEM)
     hbm = pl.BlockSpec(memory_space=pl.ANY)
     return pl.pallas_call(
         functools.partial(backward_kernel, count // 32, devices, lax.axis_size("dp")),
-        out_shape=[jax.ShapeDtypeStruct((half_rows, channels), F32)] * 2,
+        out_shape=[
+            jax.ShapeDtypeStruct((half_rows, channels), F32),
+            jax.ShapeDtypeStruct((half_rows // channels,) + region, jnp.int16),
+        ],
         in_specs=[pl.BlockSpec(memory_space=pltpu.SMEM)]
         + [vmem] * devices
         + [hbm] * 4
@@ -624,6 +634,7 @@
             pltpu.VMEM(kernels_t.shape, BF16),
             pltpu.VMEM(mix_t.shape, BF16),
             pltpu.VMEM((2 * half_rows, channels), F32),
+            pltpu.VMEM((2 * half_rows // channels,) + region, jnp.int16),
             pltpu.VMEM((rows, channels), F32),
             pltpu.VMEM(padded.shape[1:], BF16),
             pltpu.VMEM((channels, count), BF16),
@@ -686,22 +697,25 @@
     out_ref[rows:, :rows] = across.astype(jnp.int32).astype(jnp.int16)
 
 
-def decode(ref):
-    rows = ref.shape[0] - HALO
-    across = ref[rows:, :rows].astype(jnp.int32).astype(F32)
+def decode(ref, at=0, rows=None):
+    total = ref.shape[0] - HALO
+    rows = total if rows is None else rows
+    across = ref[total:, pl.ds(at, rows)].astype(jnp.int32).astype(F32)
     exponent = jnp.concatenate([across] * (LANES // HALO), axis=0).T[:, :1]
     scale = jnp.exp(exponent * np.log(2.0).astype(np.float32)) * (1.0 / 32767.0)
-    return ref[:rows, :].astype(jnp.int32).astype(F32) * scale
-
-
-def cut_kernel(size, place_ref, *refs):
-    inputs, outs = refs[:-size], refs[-size:]
-    rows = inputs[0].shape[0] // size
+    return ref[pl.ds(at, rows), :].astype(jnp.int32).astype(F32) * scale
+
+
+def cut_kernel(size, place_ref, whole_ref, *refs):
+    regions, outs = refs[:-size], refs[-size:]
+    rows = whole_ref.shape[0] // size
     for k in range(size):
         at = pl.multiple_of((place_ref[0] ^ k) * rows, rows)
-        value = inputs[0][pl.ds(at, rows), :]
-        for ref in inputs[1:]:
-            value = value + ref[pl.ds(at, rows), :]
+        value = whole_ref[pl.ds(at, rows), :]
+        for ref in regions:
+            height = ref.shape[1] - HALO
+            inside = pl.multiple_of(at % height, rows)
+            value = value + decode(ref.at[at // height], inside, rows)
         if k:
             encode(value, outs[k])
         else:
@@ -721,6 +735,12 @@
     for k, ref in enumerate(inputs):
         at = pl.multiple_of((place_ref[0] ^ k) * rows, rows)
         out_ref[pl.ds(at, rows), :] = decode(ref)
+
+
+def coded_pieces_kernel(place_ref, *refs):
+    inputs, out_ref = refs[:-1], refs[-1]
+    for k, ref in enumerate(inputs):
+        out_ref[place_ref[0] ^ k] = ref[...]
 
 
 def encode_kernel(x_ref, out_ref):
@@ -742,34 +762,40 @@
     )(*lead, *args)
 
 
-def scatter_pieces(parts, coded, axis, stride):
+def scatter_pieces(whole, regions, axis, stride):
     size = lax.axis_size(axis) // stride
     place = lax.axis_index(axis) // stride
-    rows, channels = parts[0].shape[0] // size, parts[0].shape[1]
-    if coded:
-        whole = jax.ShapeDtypeStruct(parts[0].shape, F32)
-        parts = [small_call(sum_kernel, "sum_pieces", whole, None, *parts)]
+    rows, channels = whole.shape[0] // size, whole.shape[1]
     shapes = [jax.ShapeDtypeStruct((rows, channels), F32)]
     shapes += [jax.ShapeDtypeStruct((rows + HALO, channels), jnp.int16)] * (size - 1)
     own, *others = small_call(
-        functools.partial(cut_kernel, size), "cut_pieces", shapes, place, *parts
+        functools.partial(cut_kernel, size), "cut_pieces", shapes, place, whole, *regions
     )
-    return [own] + [swap(piece, axis, (k + 1) * stride) for k, piece in enumerate(others)]
-
-
-def gather_pieces(x, axis, stride):
+    parts = [own] + [swap(piece, axis, (k + 1) * stride) for k, piece in enumerate(others)]
+    return small_call(
+        sum_kernel, "sum_pieces", jax.ShapeDtypeStruct((rows, channels), F32), None, *parts
+    )
+
+
+def gather_pieces(x, axis, stride, coded):
     size = lax.axis_size(axis) // stride
     place = lax.axis_index(axis) // stride
     rows, channels = x.shape
-    shape = jax.ShapeDtypeStruct((rows + HALO, channels), jnp.int16)
-    coded = small_call(encode_kernel, "code_piece", shape, None, x)
-    pieces = [coded] + [swap(coded, axis, k * stride) for k in range(1, size)]
-    whole = jax.ShapeDtypeStruct((size * rows, channels), F32)
-    return small_call(pieces_kernel, "lay_pieces", whole, place, *pieces)
-
-
-def spread_half(core, half_ref, is_mine, outs, sems):
+    piece = (rows + HALO, channels)
+    mine = small_call(encode_kernel, "code_piece", jax.ShapeDtypeStruct(piece, jnp.int16), None, x)
+    pieces = [mine] + [swap(mine, axis, k * stride) for k in range(1, size)]
+    if coded:
+        shape = jax.ShapeDtypeStruct((size,) + piece, jnp.int16)
+        return small_call(coded_pieces_kernel, "lay_coded_pieces", shape, place, *pieces)
+    shape = jax.ShapeDtypeStruct((size * rows, channels), F32)
+    return small_call(pieces_kernel, "lay_pieces", shape, place, *pieces)
+
+
+def spread_half(core, coded_ref, half_ref, is_mine, outs, sems):
     half_rows = half_ref.shape[0]
+    rows = half_rows // coded_ref.shape[0]
+    for k in range(coded_ref.shape[0]):
+        half_ref[k * rows : (k + 1) * rows, :] = decode(coded_ref.at[k])
     for half in range(2):
 
         @pl.when((core == half) if is_mine else (core != half))
@@ -794,42 +820,42 @@
 
 
 def spread_mine(core_ref, mine_ref, *refs):
-    spread_half(core_ref[0], mine_ref, True, refs[:-1], refs[-1])
+    *outs, half_ref, sems = refs
+    spread_half(core_ref[0], mine_ref, half_ref, True, outs, sems)
 
 
 def spread_other(classes, head_at, core_ref, mine_ref, other_ref, *refs):
-    refs = refs[(len(refs) - 3) // 2 :]
-    *outs, head_ref, loss_ref, sems = refs
-    spread_half(core_ref[0], other_ref, False, outs, sems)
-    half, at = divmod(head_at, mine_ref.shape[0])
-    mine, other = mine_ref[at : at + HALO, :], other_ref[at : at + HALO, :]
-    ends = jnp.where(core_ref[0] == half, mine, other)
+    refs = refs[(len(refs) - 4) // 2 :]
+    *outs, head_ref, loss_ref, half_ref, sems = refs
+    spread_half(core_ref[0], other_ref, half_ref, False, outs, sems)
+    half, at = divmod(head_at, half_ref.shape[0])
+    piece, inside = divmod(at, mine_ref.shape[1] - HALO)
+    mine = decode(mine_ref.at[piece])[inside : inside + HALO]
+    ends = jnp.where(core_ref[0] == half, mine, half_ref[at : at + HALO, :])
     head_ref[...] = ends[:classes]
     loss_ref[...] = ends[HALO - 1 : HALO, :1]
 
 
 def sum_everywhere(kept, sent, sizes, classes):
     core = (lax.axis_index("dp") % 2).reshape(1).astype(jnp.int32)
-    parts = scatter_pieces([kept, swap(sent, "dp", 1)], False, "dp", 2)
-    parts = scatter_pieces(parts, True, "freq", 1)
-    x = small_call(
-        sum_kernel, "sum_pieces", jax.ShapeDtypeStruct(parts[0].shape, F32), None, *parts
-    )
-    x = gather_pieces(x, "freq", 1)
-    x = gather_pieces(x, "dp", 2)
+    x = scatter_pieces(kept, [swap(sent, "dp", 1)], "dp", 2)
+    x = scatter_pieces(x, [], "freq", 1)
+    x = gather_pieces(x, "freq", 1, False)
+    x = gather_pieces(x, "dp", 2, True)
     other = swap(x, "dp", 1)
-    channels = x.shape[1]
+    channels = x.shape[2]
     shapes = [jax.ShapeDtypeStruct((rows, channels), F32) for rows in sizes[:-1]]
     hbm = pl.BlockSpec(memory_space=pl.ANY)
     vmem = pl.BlockSpec(memory_space=pltpu.VMEM)
     smem = pl.BlockSpec(memory_space=pltpu.SMEM)
-    sems = [pltpu.SemaphoreType.DMA((len(sizes),))]
+    scratch = [pltpu.VMEM(kept.shape, F32), pltpu.SemaphoreType.DMA((len(sizes),))]
     halves = pl.pallas_call(
         spread_mine,
         out_shape=shapes,
         in_specs=[smem, vmem],
         out_specs=[hbm] * len(shapes),
-        scratch_shapes=sems,
+        scratch_shapes=scratch,
+        compiler_params=pltpu.CompilerParams(vmem_limit_bytes=32 * 1024 * 1024),
         cost_estimate=pl.CostEstimate(flops=0, bytes_accessed=2**23, transcendentals=0),
         name="spread_mine",
     )(core, x)
@@ -842,26 +868,15 @@
         ],
         in_specs=[smem, vmem, vmem] + [hbm] * len(shapes),
         out_specs=[hbm] * len(shapes) + [vmem] * 2,
-        scratch_shapes=sems,
+        scratch_shapes=scratch,
         input_output_aliases={3 + k: k for k in range(len(shapes))},
+        compiler_params=pltpu.CompilerParams(vmem_limit_bytes=32 * 1024 * 1024),
         name="spread_other",
     )(core, x, other, *halves)
 
 
-def shifted(pieces, axis):
-    size = len(pieces)
-    return [pieces[0]] + [
-        lax.ppermute(pieces[k], axis, [(i, (i + k) % size) for i in range(size)])
-        for k in range(1, size)
-    ]
-
-
-def all_of(x, axis):
-    size = lax.axis_size(axis)
-    pieces = [x]
-    for shift in range(1, size):
-        pieces.append(lax.ppermute(x, axis, [(i, (i + shift) % size) for i in range(size)]))
-    return pieces
+def traded(pieces, axis):
+    return [pieces[0]] + [swap(pieces[k], axis, k) for k in range(1, len(pieces))]
 
 
 def local(records, stem_weight, conv_weight, mix_weight, head_weight, labels, band_bounds):
@@ -884,12 +899,13 @@
     sent = [
         first_section(here, records[0], c, signals, freq, section, twiddle) for c in range(chunks)
     ]
-    arrived = [shifted(pieces, "freq") for pieces in sent]
+    arrived = [traded(pieces, "freq") for pieces in sent]
+    dense = dense_weights(conv_weight, mix_weight)
+    arrived[0], (kernels, kernels_t, mix_t) = lax.optimization_barrier((arrived[0], dense))
     features = [
         second_section(here, a, second_len, total_len, spread, table, flip) for a in arrived
     ]
-    received = [piece for f in features for piece in shifted(f, "freq")]
-    kernels, kernels_t, mix_t = dense_weights(conv_weight, mix_weight)
+    received = [piece for f in features for piece in traded(f, "freq")]
     head_t = jnp.pad(head_weight.T, ((0, HALO - classes), (0, 0)))
     steps = jnp.repeat(band_bounds // POOL, GROUP_WIDTH)
     bounds = jnp.stack([steps[:channels], steps[GROUP_WIDTH:]]).astype(jnp.int32)
@@ -924,7 +940,7 @@
         name="network_ahead",
     )(here, *received, stem_weight, kernels, mix_weight, bounds)
 
-    sums = all_of(partial, "freq")
+    sums = traded([partial] * freq, "freq")
     core = (lax.axis_index("dp") % 2).astype(jnp.int32)
     scalars = jnp.stack([place, labels[0], jnp.int32(classes), core])
     sizes = [layers * channels, 2 * LANES, layers * KW * GROUP_WIDTH, HALO]

time: 224 us -> 208 us (0.929); the launches traced: 222 us -> 204 us
  starting transfers between devices: 66.5 us -> 54.6 us
  waiting for transfers between devices: 46.3 us -> 42.7 us
    ppermute x15 -> x0, starting transfers between devices: 50.4 us -> none  [the longest x12 35.2 us: shifted(): lax.ppermute(pieces[k], axis, [(i, (i + k) % size) for i in range(size)])]
    ppermute x14 -> x29, starting transfers between devices: 16.1 us -> 54.6 us  [swap(): lax.ppermute(x, axis, [(i, i ^ step) for i in range(lax.axis_size(axis))])]
    ppermute x15 -> x0, waiting for transfers between devices: 10 us -> none  [the longest x12 5.67 us: shifted(): lax.ppermute(pieces[k], axis, [(i, (i + k) % size) for i in range(size)])]
    ppermute x14 -> x29, waiting for transfers between devices: 36.3 us -> 42.7 us  [swap(): lax.ppermute(x, axis, [(i, i ^ step) for i in range(lax.axis_size(axis))])]
    unnamed x52 -> x50, local copies, waits for them, and re-layouts: 12.5 us -> 11.2 us
  transfers between devices with their start and end apart: 29 -> 29, of which waited for: 13 -> 15; matrix products, arithmetic and copies ran while one was open for 1% -> 1% of each run, Pallas kernels for 13% -> 14%
where the time goes in v1:
time: 208 us; the launch traced here: 204 us
  Pallas kernels  91.7 us (44%)
  starting transfers between devices  54.6 us (26%)
  waiting for transfers between devices  42.7 us (21%)
  local copies, waits for them, and re-layouts  12.2 us (6%)
    ppermute x29, starting transfers between devices, swap(): lax.ppermute(x, axis, [(i, i ^ step) for i in range(lax.axis_size(axis))])  54.6 us
    ppermute x29, waiting for transfers between devices, swap(): lax.ppermute(x, axis, [(i, i ^ step) for i in range(lax.axis_size(axis))])  42.7 us
    pallas_call x1, Pallas kernels, network_back(): pl.pallas_call(functools.partial(backward_kernel, count // 32, devices, l...  32 us
    pallas_call x1, Pallas kernels, local(): pl.pallas_call(functools.partial(forward_kernel, run, freq, chunks), out_...  17.6 us
    pallas_call x2, Pallas kernels, first_section(): pl.pallas_call(functools.partial(first_kernel, devices), out_shape=[jax.S...  17.4 us
    pallas_call x2, Pallas kernels, second_section(): pl.pallas_call(functools.partial(second_kernel, devices, total_len), out_...  16.4 us
    unnamed x50, local copies, waits for them, and re-layouts  11.2 us
  transfers between devices with their start and end apart: 29, of which 15 were waited for; matrix products, arithmetic and copies ran while one was open for 1% of the time, Pallas kernels for 14%

profile of v1, /device:TPU:0, one launch (start us, length us, event | category | flops | bytes accessed | tf_op | source)
XLA Modules:
  0.0 204.1 jit_solution(8130692788960167606)
XLA Ops:
  0.6 8.6 %first_section.2 = (s16[528,256]{1,0:T(8,128)(2,1)}, s16[528,256]{1,0:T(8,128)(2,1)}, s16[528,256]{1,0:T(8,128)(2,1)}, s16[528,256]{1,0:T(8,128)(2,1)}) custom-call(s32[1]{0:T(128)} %bitcast.2.place_ref, f32[2,1024,512]{2,1,0:T(8,128)} %bitcast.9, bf16[2,1024,1024]{2,1,0:T(8,128)(2,1)} %constant.76.clone.table_ref, f32[2048,1024]{1,0:T(8,128)} %constant.77.clone.twiddle_ref), custom_call_target="tpu_custom_call" | custom-call | flops 3221225472 | bytes 8388608 | tf_op jit(solution)/shard_map/first_section/pallas_call | solution.py:107
  9.3 3.0 %collective-permute-start = (s16[528,256]{1,0:T(8,128)(2,1)}, s16[528,256]{1,0:T(8,128)(2,1)S(1)}, u32[]{:S(2)}, u32[]{:S(2)}) collective-permute-start(s16[528,256]{1,0:T(8,128)(2,1)} %get-tuple-element.55), channel_id=1, source_target_pairs={{0,1},{1,0},{2,3},{3,2},{4,5},{5,4},{6,7},{7,6},{8,9},{9,8},{10,11... | collective-permute-start | bytes 811016 | tf_op jit(solution)/shard_map/ppermute | solution.py:686
  12.3 2.6 %collective-permute-start.1 = (s16[528,256]{1,0:T(8,128)(2,1)}, s16[528,256]{1,0:T(8,128)(2,1)S(1)}, u32[]{:S(2)}, u32[]{:S(2)}) collective-permute-start(s16[528,256]{1,0:T(8,128)(2,1)} %get-tuple-element.56), channel_id=1, source_target_pairs={{0,2},{1,3},{2,0},{3,1},{4,6},{5,7},{6,4},{7,5},{8,10},{9,11},{10,... | collective-permute-start | bytes 811016 | tf_op jit(solution)/shard_map/ppermute | solution.py:686
  15.0 8.7 %first_section.3 = (s16[528,256]{1,0:T(8,128)(2,1)}, s16[528,256]{1,0:T(8,128)(2,1)}, s16[528,256]{1,0:T(8,128)(2,1)}, s16[528,256]{1,0:T(8,128)(2,1)}) custom-call(s32[1]{0:T(128)} %bitcast.2.place_ref, f32[2,1024,512]{2,1,0:T(8,128)} %bitcast.10, bf16[2,1024,1024]{2,1,0:T(8,128)(2,1)} %constant.76.clone.table_ref, f32[2048,1024]{1,0:T(8,128)} %constant.77.clone.twiddle_ref), custom_call_target="tpu_custom_call" | custom-call | flops 3221225472 | bytes 8388608 | tf_op jit(solution)/shard_map/first_section/pallas_call | solution.py:107
  24.6 3.4 %collective-permute-start.7 = (s16[528,256]{1,0:T(8,128)(2,1)}, s16[528,256]{1,0:T(8,128)(2,1)S(1)}, u32[]{:S(2)}, u32[]{:S(2)}) collective-permute-start(s16[528,256]{1,0:T(8,128)(2,1)} %get-tuple-element.71), channel_id=1, source_target_pairs={{0,2},{1,3},{2,0},{3,1},{4,6},{5,7},{6,4},{7,5},{8,10},{9,11},{10,... | collective-permute-start | bytes 811016 | tf_op jit(solution)/shard_map/ppermute | solution.py:686
  28.0 1.5 dense_weights.1
  34.5 1.6 copy-done.10
  37.5 8.2 %second_section.2 = (bf16[528,128]{1,0:T(8,128)(2,1)S(1)}, bf16[528,128]{1,0:T(8,128)(2,1)S(1)}, bf16[528,128]{1,0:T(8,128)(2,1)S(1)}, bf16[528,128]{1,0:T(8,128)(2,1)S(1)}) custom-call(s32[1]{0:T(128)} %bitcast.2.place_ref, s16[528,256]{1,0:T(8,128)(2,1)S(1)} %copy-done.9, s16[528,256]{1,0:T(8,128)(2,1)S(1)} %collective-permute-done.refs_1_, ...), custom_call_target="tpu_custom_call" | custom-call | flops 3221225472 | bytes 8388608 | tf_op jit(solution)/shard_map/second_section/pallas_call | solution.py:212
  46.3 17.9 %collective-permute-start.3 = (bf16[528,128]{1,0:T(8,128)(2,1)S(1)}, bf16[528,128]{1,0:T(8,128)(2,1)S(1)}, u32[]{:S(2)}, u32[]{:S(2)}) collective-permute-start(bf16[528,128]{1,0:T(8,128)(2,1)S(1)} %get-tuple-element.66), channel_id=1, source_target_pairs={{0,1},{1,0},{2,3},{3,2},{4,5},{5,4},{6,7},{7,6},{8,9},{9,8},{10,11... | collective-permute-start | bytes 405512 | tf_op jit(solution)/shard_map/ppermute | solution.py:686
  66.8 8.2 %second_section.3 = (bf16[528,128]{1,0:T(8,128)(2,1)S(1)}, bf16[528,128]{1,0:T(8,128)(2,1)S(1)}, bf16[528,128]{1,0:T(8,128)(2,1)S(1)}, bf16[528,128]{1,0:T(8,128)(2,1)S(1)}) custom-call(s32[1]{0:T(128)} %bitcast.2.place_ref, s16[528,256]{1,0:T(8,128)(2,1)S(1)} %copy-done.8, s16[528,256]{1,0:T(8,128)(2,1)S(1)} %collective-permute-done.6.refs_1_, ...), custom_call_target="tpu_custom_call" | custom-call | flops 3221225472 | bytes 8388608 | tf_op jit(solution)/shard_map/second_section/pallas_call | solution.py:212
  75.7 2.0 collective-permute-start.10
  80.8 4.3 %collective-permute-done.10.refs_6_ = bf16[528,128]{1,0:T(8,128)(2,1)S(1)} collective-permute-done((bf16[528,128]{1,0:T(8,128)(2,1)S(1)}, bf16[528,128]{1,0:T(8,128)(2,1)S(1)}, u32[]{:S(2)}, u32[]{:S(2)}) %collective-permute-start.10) | collective-permute-done | bytes 135200 | tf_op jit(solution)/shard_map/ppermute | solution.py:686
  87.1 17.6 %network_ahead.1 = (f32[3,2064,512]{2,1,0:T(8,128)}, f32[3,2064,128]{2,1,0:T(8,128)}, bf16[3,2192,512]{2,1,0:T(8,128)(2,1)}, bf16[2064,256]{1,0:T(8,128)(2,1)}, f32[8,512]{1,0:T(8,128)}) custom-call(s32[1]{0:T(128)} %bitcast.2.place_ref, bf16[528,128]{1,0:T(8,128)(2,1)} %copy-done.6, bf16[528,128]{1,0:T(8,128)(2,1)} %copy-done.14, ...), custom_call_target="tpu_custom_call" | custom-call | tf_op jit(solution)/shard_map/network_ahead/pallas_call | solution.py:922
  105.5 1.8 collective-permute-start.13
  107.3 1.8 collective-permute-start.14
  110.4 2.7 %collective-permute-done.14.refs_3_ = f32[8,512]{1,0:T(8,128)S(1)} collective-permute-done((f32[8,512]{1,0:T(8,128)}, f32[8,512]{1,0:T(8,128)S(1)}, u32[]{:S(2)}, u32[]{:S(2)}) %collective-permute-start.14) | collective-permute-done | bytes 16416 | tf_op jit(solution)/shard_map/ppermute | solution.py:686
  113.7 32.0 %network_back.1 = (f32[1024,512]{1,0:T(8,128)}, s16[2,528,512]{2,1,0:T(8,128)(2,1)}) custom-call(s32[4]{0:T(128)} %pad_add_fusion.1.place_ref, f32[8,512]{1,0:T(8,128)} %get-tuple-element.78.refs_0_, f32[8,512]{1,0:T(8,128)} %copy-done.21, f32[8,512]{1,0:T(8,128)} %copy-done.22, f32[8,512]{1,0:T(8,128)} %copy-done.23, ...), custom_call_target="tpu_custom_call" | custom-call | tf_op jit(solution)/shard_map/network_back/pallas_call | solution.py:620
  145.8 2.9 %collective-permute-done.15.refs_0_ = s16[2,528,512]{2,1,0:T(8,128)(2,1)S(1)} collective-permute-done((s16[2,528,512]{2,1,0:T(8,128)(2,1)}, s16[2,528,512]{2,1,0:T(8,128)(2,1)S(1)}, u32[]{:S(2)}, u32[]{:S(2)}) %collective-permute-start.15) | collective-permute-done | bytes 1081376 | tf_op jit(solution)/shard_map/ppermute | solution.py:686
  148.7 1.6 copy-done.3
  151.4 1.5 collective-permute-start.16
  153.0 1.5 collective-permute-start.17
  155.0 6.0 %collective-permute-done.16.refs_0_ = s16[272,512]{1,0:T(8,128)(2,1)S(1)} collective-permute-done((s16[272,512]{1,0:T(8,128)(2,1)S(1)}, s16[272,512]{1,0:T(8,128)(2,1)S(1)}, u32[]{:S(2)}, u32[]{:S(2)}) %collective-permute-start.16) | collective-permute-done | bytes 278560 | tf_op jit(solution)/shard_map/ppermute | solution.py:686
  161.0 6.4 %collective-permute-done.17.refs_1_ = s16[272,512]{1,0:T(8,128)(2,1)S(1)} collective-permute-done((s16[272,512]{1,0:T(8,128)(2,1)S(1)}, s16[272,512]{1,0:T(8,128)(2,1)S(1)}, u32[]{:S(2)}, u32[]{:S(2)}) %collective-permute-start.17) | collective-permute-done | bytes 278560 | tf_op jit(solution)/shard_map/ppermute | solution.py:686
  168.0 2.4 %collective-permute-start.20 = (s16[80,512]{1,0:T(8,128)(2,1)S(1)}, s16[80,512]{1,0:T(8,128)(2,1)S(1)}, u32[]{:S(2)}, u32[]{:S(2)}) collective-permute-start(s16[80,512]{1,0:T(8,128)(2,1)S(1)} %get-tuple-element.93), channel_id=1, source_target_pairs={{0,2},{1,3},{2,0},{3,1},{4,6},{5,7},{6,4},{7,5},{8,10},{9,11},{10,... | collective-permute-start | bytes 245768 | tf_op jit(solution)/shard_map/ppermute | solution.py:686
  170.4 1.9 collective-permute-start.21
  172.4 4.4 %collective-permute-done.20.refs_1_ = s16[80,512]{1,0:T(8,128)(2,1)S(1)} collective-permute-done((s16[80,512]{1,0:T(8,128)(2,1)S(1)}, s16[80,512]{1,0:T(8,128)(2,1)S(1)}, u32[]{:S(2)}, u32[]{:S(2)}) %collective-permute-start.20) | collective-permute-done | bytes 81952 | tf_op jit(solution)/shard_map/ppermute | solution.py:686
  179.7 1.9 collective-permute-start.24
  182.9 2.0 collective-permute-done.23.refs_2_
  190.0 4.2 %collective-permute-done.25.refs_1_ = s16[272,512]{1,0:T(8,128)(2,1)S(1)} collective-permute-done((s16[272,512]{1,0:T(8,128)(2,1)S(1)}, s16[272,512]{1,0:T(8,128)(2,1)S(1)}, u32[]{:S(2)}, u32[]{:S(2)}) %collective-permute-start.25) | collective-permute-done | bytes 278560 | tf_op jit(solution)/shard_map/ppermute | solution.py:686
  194.2 4.4 %collective-permute-done.26.refs_2_ = s16[272,512]{1,0:T(8,128)(2,1)S(1)} collective-permute-done((s16[272,512]{1,0:T(8,128)(2,1)S(1)}, s16[272,512]{1,0:T(8,128)(2,1)S(1)}, u32[]{:S(2)}, u32[]{:S(2)}) %collective-permute-start.26) | collective-permute-done | bytes 278560 | tf_op jit(solution)/shard_map/ppermute | solution.py:686
  198.7 1.8 spread_mine.1
  201.5 2.4 %spread_other.1 = (f32[1536,512]{1,0:T(8,128)}, f32[256,512]{1,0:T(8,128)}, f32[144,512]{1,0:T(8,128)}, f32[10,512]{1,0:T(8,128)}, f32[1,1]{1,0:T(1,128)}) custom-call(s32[1]{0:T(128)} %bitcast.core_ref, s16[4,272,512]{2,1,0:T(8,128)(2,1)S(1)} %lay_coded_pieces.1.mine_ref, ...), custom_call_target="tpu_custom_call", output_to_operand_aliasing={{0}: (3, {}), {1}: (4, {}), {2}: (5, {})} | custom-call | tf_op jit(solution)/shard_map/spread_other/pallas_call | solution.py:862
  (102 shorter events, 30.9 us)
Async XLA Ops:
  9.3 24.3 %collective-permute-start = (s16[528,256]{1,0:T(8,128)(2,1)}, s16[528,256]{1,0:T(8,128)(2,1)S(1)}, u32[]{:S(2)}, u32[]{:S(2)}) collective-permute-start(s16[528,256]{1,0:T(8,128)(2,1)} %get-tuple-element.55), channel_id=1, source_target_pairs={{0,1},{1,0},{2,3},{3,2},{4,5},{5,4},{6,7},{7,6},{8,9},{9,8},{10,11... | collective-permute-start | bytes 811016 | tf_op jit(solution)/shard_map/ppermute | solution.py:686
  12.3 22.1 %collective-permute-start.1 = (s16[528,256]{1,0:T(8,128)(2,1)}, s16[528,256]{1,0:T(8,128)(2,1)S(1)}, u32[]{:S(2)}, u32[]{:S(2)}) collective-permute-start(s16[528,256]{1,0:T(8,128)(2,1)} %get-tuple-element.56), channel_id=1, source_target_pairs={{0,2},{1,3},{2,0},{3,1},{4,6},{5,7},{6,4},{7,5},{8,10},{9,11},{10,... | collective-permute-start | bytes 811016 | tf_op jit(solution)/shard_map/ppermute | solution.py:686
  14.9 19.5 %collective-permute-start.2 = (s16[528,256]{1,0:T(8,128)(2,1)}, s16[528,256]{1,0:T(8,128)(2,1)S(1)}, u32[]{:S(2)}, u32[]{:S(2)}) collective-permute-start(s16[528,256]{1,0:T(8,128)(2,1)} %get-tuple-element.57), channel_id=1, source_target_pairs={{0,3},{1,2},{2,1},{3,0},{4,7},{5,6},{6,5},{7,4},{8,11},{9,10},{10,... | collective-permute-start | bytes 811016 | tf_op jit(solution)/shard_map/ppermute | solution.py:686
  23.7 41.6 %collective-permute-start.6 = (s16[528,256]{1,0:T(8,128)(2,1)}, s16[528,256]{1,0:T(8,128)(2,1)S(1)}, u32[]{:S(2)}, u32[]{:S(2)}) collective-permute-start(s16[528,256]{1,0:T(8,128)(2,1)} %get-tuple-element.70), channel_id=1, source_target_pairs={{0,1},{1,0},{2,3},{3,2},{4,5},{5,4},{6,7},{7,6},{8,9},{9,8},{10,11... | collective-permute-start | bytes 811016 | tf_op jit(solution)/shard_map/ppermute | solution.py:686
  24.6 42.2 %collective-permute-start.7 = (s16[528,256]{1,0:T(8,128)(2,1)}, s16[528,256]{1,0:T(8,128)(2,1)S(1)}, u32[]{:S(2)}, u32[]{:S(2)}) collective-permute-start(s16[528,256]{1,0:T(8,128)(2,1)} %get-tuple-element.71), channel_id=1, source_target_pairs={{0,2},{1,3},{2,0},{3,1},{4,6},{5,7},{6,4},{7,5},{8,10},{9,11},{10,... | collective-permute-start | bytes 811016 | tf_op jit(solution)/shard_map/ppermute | solution.py:686
  33.6 33.2 %collective-permute-start.8 = (s16[528,256]{1,0:T(8,128)(2,1)}, s16[528,256]{1,0:T(8,128)(2,1)S(1)}, u32[]{:S(2)}, u32[]{:S(2)}) collective-permute-start(s16[528,256]{1,0:T(8,128)(2,1)} %get-tuple-element.72), channel_id=1, source_target_pairs={{0,3},{1,2},{2,1},{3,0},{4,7},{5,6},{6,5},{7,4},{8,11},{9,10},{10,... | collective-permute-start | bytes 811016 | tf_op jit(solution)/shard_map/ppermute | solution.py:686
  37.5 29.3 %copy-start.8 = (s16[528,256]{1,0:T(8,128)(2,1)S(1)}, s16[528,256]{1,0:T(8,128)(2,1)}, u32[]{:S(2)}) copy-start(s16[528,256]{1,0:T(8,128)(2,1)} %get-tuple-element.69.refs_0_) | copy-start | bytes 811012
  37.5 29.3 %copy-start.11 = (bf16[2,512,1024]{2,1,0:T(8,128)(2,1)S(1)}, bf16[2,512,1024]{2,1,0:T(8,128)(2,1)}, u32[]{:S(2)}) copy-start(bf16[2,512,1024]{2,1,0:T(8,128)(2,1)} %constant.79.clone.refs_5_) | copy-start | bytes 6291460
  46.3 32.7 %collective-permute-start.3 = (bf16[528,128]{1,0:T(8,128)(2,1)S(1)}, bf16[528,128]{1,0:T(8,128)(2,1)S(1)}, u32[]{:S(2)}, u32[]{:S(2)}) collective-permute-start(bf16[528,128]{1,0:T(8,128)(2,1)S(1)} %get-tuple-element.66), channel_id=1, source_target_pairs={{0,1},{1,0},{2,3},{3,2},{4,5},{5,4},{6,7},{7,6},{8,9},{9,8},{10,11... | collective-permute-start | bytes 405512 | tf_op jit(solution)/shard_map/ppermute | solution.py:686
  64.3 16.5 %collective-permute-start.4 = (bf16[528,128]{1,0:T(8,128)(2,1)S(1)}, bf16[528,128]{1,0:T(8,128)(2,1)S(1)}, u32[]{:S(2)}, u32[]{:S(2)}) collective-permute-start(bf16[528,128]{1,0:T(8,128)(2,1)S(1)} %get-tuple-element.67), channel_id=1, source_target_pairs={{0,2},{1,3},{2,0},{3,1},{4,6},{5,7},{6,4},{7,5},{8,10},{9,11},{10,... | collective-permute-start | bytes 405512 | tf_op jit(solution)/shard_map/ppermute | solution.py:686
  65.3 15.5 %collective-permute-start.5 = (bf16[528,128]{1,0:T(8,128)(2,1)S(1)}, bf16[528,128]{1,0:T(8,128)(2,1)S(1)}, u32[]{:S(2)}, u32[]{:S(2)}) collective-permute-start(bf16[528,128]{1,0:T(8,128)(2,1)S(1)} %get-tuple-element.68), channel_id=1, source_target_pairs={{0,3},{1,2},{2,1},{3,0},{4,7},{5,6},{6,5},{7,4},{8,11},{9,10},{10,... | collective-permute-start | bytes 405512 | tf_op jit(solution)/shard_map/ppermute | solution.py:686
  75.7 9.5 %collective-permute-start.10 = (bf16[528,128]{1,0:T(8,128)(2,1)S(1)}, bf16[528,128]{1,0:T(8,128)(2,1)S(1)}, u32[]{:S(2)}, u32[]{:S(2)}) collective-permute-start(bf16[528,128]{1,0:T(8,128)(2,1)S(1)} %get-tuple-element.75), channel_id=1, source_target_pairs={{0,2},{1,3},{2,0},{3,1},{4,6},{5,7},{6,4},{7,5},{8,10},{9,11},{10,... | collective-permute-start | bytes 405512 | tf_op jit(solution)/shard_map/ppermute | solution.py:686
  77.7 7.5 %collective-permute-start.11 = (bf16[528,128]{1,0:T(8,128)(2,1)S(1)}, bf16[528,128]{1,0:T(8,128)(2,1)S(1)}, u32[]{:S(2)}, u32[]{:S(2)}) collective-permute-start(bf16[528,128]{1,0:T(8,128)(2,1)S(1)} %get-tuple-element.76), channel_id=1, source_target_pairs={{0,3},{1,2},{2,1},{3,0},{4,7},{5,6},{6,5},{7,4},{8,11},{9,10},{10,... | collective-permute-start | bytes 405512 | tf_op jit(solution)/shard_map/ppermute | solution.py:686
  79.1 7.4 %collective-permute-start.9 = (bf16[528,128]{1,0:T(8,128)(2,1)S(1)}, bf16[528,128]{1,0:T(8,128)(2,1)S(1)}, u32[]{:S(2)}, u32[]{:S(2)}) collective-permute-start(bf16[528,128]{1,0:T(8,128)(2,1)S(1)} %get-tuple-element.74), channel_id=1, source_target_pairs={{0,1},{1,0},{2,3},{3,2},{4,5},{5,4},{6,7},{7,6},{8,9},{9,8},{10,11... | collective-permute-start | bytes 405512 | tf_op jit(solution)/shard_map/ppermute | solution.py:686
  87.1 22.6 %copy-start.20 = (f32[512,10]{0,1:T(8,128)S(1)}, f32[512,10]{0,1:T(8,128)}, u32[]{:S(2)}) copy-start(f32[512,10]{0,1:T(8,128)} %param.16) | copy-start | bytes 61444
  104.7 5.7 %collective-permute-start.12 = (f32[8,512]{1,0:T(8,128)}, f32[8,512]{1,0:T(8,128)S(1)}, u32[]{:S(2)}, u32[]{:S(2)}) collective-permute-start(f32[8,512]{1,0:T(8,128)} %get-tuple-element.78.refs_0_), channel_id=1, source_target_pairs={{0,1},{1,0},{2,3},{3,2},{4,5},{5,4},{6,7},{7,6},{8,9},{9,8},{10,11... | collective-permute-start | bytes 49160 | tf_op jit(solution)/shard_map/ppermute | solution.py:686
  105.5 4.9 %collective-permute-start.13 = (f32[8,512]{1,0:T(8,128)}, f32[8,512]{1,0:T(8,128)S(1)}, u32[]{:S(2)}, u32[]{:S(2)}) collective-permute-start(f32[8,512]{1,0:T(8,128)} %get-tuple-element.78.refs_0_), channel_id=1, source_target_pairs={{0,2},{1,3},{2,0},{3,1},{4,6},{5,7},{6,4},{7,5},{8,10},{9,11},{10,... | collective-permute-start | bytes 49160 | tf_op jit(solution)/shard_map/ppermute | solution.py:686
  107.3 5.7 %collective-permute-start.14 = (f32[8,512]{1,0:T(8,128)}, f32[8,512]{1,0:T(8,128)S(1)}, u32[]{:S(2)}, u32[]{:S(2)}) collective-permute-start(f32[8,512]{1,0:T(8,128)} %get-tuple-element.78.refs_0_), channel_id=1, source_target_pairs={{0,3},{1,2},{2,1},{3,0},{4,7},{5,6},{6,5},{7,4},{8,11},{9,10},{10,... | collective-permute-start | bytes 49160 | tf_op jit(solution)/shard_map/ppermute | solution.py:686
  145.7 3.0 %collective-permute-start.15 = (s16[2,528,512]{2,1,0:T(8,128)(2,1)}, s16[2,528,512]{2,1,0:T(8,128)(2,1)S(1)}, u32[]{:S(2)}, u32[]{:S(2)}) collective-permute-start(s16[2,528,512]{2,1,0:T(8,128)(2,1)} %get-tuple-element.86), channel_id=1, source_target_pairs={{0,4},{4,0},{8,12},{12,8},{16,20},{20,16},{24,28},{28,24},{1,5},{5... | collective-permute-start | bytes 3244040 | tf_op jit(solution)/shard_map/ppermute | solution.py:686
  151.4 9.5 %collective-permute-start.16 = (s16[272,512]{1,0:T(8,128)(2,1)S(1)}, s16[272,512]{1,0:T(8,128)(2,1)S(1)}, u32[]{:S(2)}, u32[]{:S(2)}) collective-permute-start(s16[272,512]{1,0:T(8,128)(2,1)S(1)} %get-tuple-element.88), channel_id=1, source_target_pairs={{0,8},{4,12},{8,0},{12,4},{16,24},{20,28},{24,16},{28,20},{1,9},{5... | collective-permute-start | bytes 835592 | tf_op jit(solution)/shard_map/ppermute | solution.py:686
  153.0 14.4 %collective-permute-start.17 = (s16[272,512]{1,0:T(8,128)(2,1)S(1)}, s16[272,512]{1,0:T(8,128)(2,1)S(1)}, u32[]{:S(2)}, u32[]{:S(2)}) collective-permute-start(s16[272,512]{1,0:T(8,128)(2,1)S(1)} %get-tuple-element.89), channel_id=1, source_target_pairs={{0,16},{4,20},{8,24},{12,28},{16,0},{20,4},{24,8},{28,12},{1,17},{... | collective-permute-start | bytes 835592 | tf_op jit(solution)/shard_map/ppermute | solution.py:686
  154.5 12.9 %collective-permute-start.18 = (s16[272,512]{1,0:T(8,128)(2,1)S(1)}, s16[272,512]{1,0:T(8,128)(2,1)S(1)}, u32[]{:S(2)}, u32[]{:S(2)}) collective-permute-start(s16[272,512]{1,0:T(8,128)(2,1)S(1)} %get-tuple-element.90), channel_id=1, source_target_pairs={{0,24},{4,28},{8,16},{12,20},{16,8},{20,12},{24,0},{28,4},{1,25},{... | collective-permute-start | bytes 835592 | tf_op jit(solution)/shard_map/ppermute | solution.py:686
  168.0 4.5 %collective-permute-start.19 = (s16[80,512]{1,0:T(8,128)(2,1)S(1)}, s16[80,512]{1,0:T(8,128)(2,1)S(1)}, u32[]{:S(2)}, u32[]{:S(2)}) collective-permute-start(s16[80,512]{1,0:T(8,128)(2,1)S(1)} %get-tuple-element.92), channel_id=1, source_target_pairs={{0,1},{1,0},{2,3},{3,2},{4,5},{5,4},{6,7},{7,6},{8,9},{9,8},{10,11... | collective-permute-start | bytes 245768 | tf_op jit(solution)/shard_map/ppermute | solution.py:686
  168.0 8.8 %collective-permute-start.20 = (s16[80,512]{1,0:T(8,128)(2,1)S(1)}, s16[80,512]{1,0:T(8,128)(2,1)S(1)}, u32[]{:S(2)}, u32[]{:S(2)}) collective-permute-start(s16[80,512]{1,0:T(8,128)(2,1)S(1)} %get-tuple-element.93), channel_id=1, source_target_pairs={{0,2},{1,3},{2,0},{3,1},{4,6},{5,7},{6,4},{7,5},{8,10},{9,11},{10,... | collective-permute-start | bytes 245768 | tf_op jit(solution)/shard_map/ppermute | solution.py:686
  170.4 6.4 %collective-permute-start.21 = (s16[80,512]{1,0:T(8,128)(2,1)S(1)}, s16[80,512]{1,0:T(8,128)(2,1)S(1)}, u32[]{:S(2)}, u32[]{:S(2)}) collective-permute-start(s16[80,512]{1,0:T(8,128)(2,1)S(1)} %get-tuple-element.94), channel_id=1, source_target_pairs={{0,3},{1,2},{2,1},{3,0},{4,7},{5,6},{6,5},{7,4},{8,11},{9,10},{10,... | collective-permute-start | bytes 245768 | tf_op jit(solution)/shard_map/ppermute | solution.py:686
  177.2 5.7 %collective-permute-start.22 = (s16[80,512]{1,0:T(8,128)(2,1)S(1)}, s16[80,512]{1,0:T(8,128)(2,1)S(1)}, u32[]{:S(2)}, u32[]{:S(2)}) collective-permute-start(s16[80,512]{1,0:T(8,128)(2,1)S(1)} %code_piece.2.refs_0_), channel_id=1, source_target_pairs={{0,1},{1,0},{2,3},{3,2},{4,5},{5,4},{6,7},{7,6},{8,9},{9,8},{10,11... | collective-permute-start | bytes 245768 | tf_op jit(solution)/shard_map/ppermute | solution.py:686
  178.6 6.2 %collective-permute-start.23 = (s16[80,512]{1,0:T(8,128)(2,1)S(1)}, s16[80,512]{1,0:T(8,128)(2,1)S(1)}, u32[]{:S(2)}, u32[]{:S(2)}) collective-permute-start(s16[80,512]{1,0:T(8,128)(2,1)S(1)} %code_piece.2.refs_0_), channel_id=1, source_target_pairs={{0,2},{1,3},{2,0},{3,1},{4,6},{5,7},{6,4},{7,5},{8,10},{9,11},{10,... | collective-permute-start | bytes 245768 | tf_op jit(solution)/shard_map/ppermute | solution.py:686
  179.7 6.3 %collective-permute-start.24 = (s16[80,512]{1,0:T(8,128)(2,1)S(1)}, s16[80,512]{1,0:T(8,128)(2,1)S(1)}, u32[]{:S(2)}, u32[]{:S(2)}) collective-permute-start(s16[80,512]{1,0:T(8,128)(2,1)S(1)} %code_piece.2.refs_0_), channel_id=1, source_target_pairs={{0,3},{1,2},{2,1},{3,0},{4,7},{5,6},{6,5},{7,4},{8,11},{9,10},{10,... | collective-permute-start | bytes 245768 | tf_op jit(solution)/shard_map/ppermute | solution.py:686
  186.4 7.7 %collective-permute-start.25 = (s16[272,512]{1,0:T(8,128)(2,1)S(1)}, s16[272,512]{1,0:T(8,128)(2,1)S(1)}, u32[]{:S(2)}, u32[]{:S(2)}) collective-permute-start(s16[272,512]{1,0:T(8,128)(2,1)S(1)} %code_piece.3.refs_0_), channel_id=1, source_target_pairs={{0,8},{4,12},{8,0},{12,4},{16,24},{20,28},{24,16},{28,20},{1,9},{5... | collective-permute-start | bytes 835592 | tf_op jit(solution)/shard_map/ppermute | solution.py:686
  187.9 10.7 %collective-permute-start.26 = (s16[272,512]{1,0:T(8,128)(2,1)S(1)}, s16[272,512]{1,0:T(8,128)(2,1)S(1)}, u32[]{:S(2)}, u32[]{:S(2)}) collective-permute-start(s16[272,512]{1,0:T(8,128)(2,1)S(1)} %code_piece.3.refs_0_), channel_id=1, source_target_pairs={{0,16},{4,20},{8,24},{12,28},{16,0},{20,4},{24,8},{28,12},{1,17},{... | collective-permute-start | bytes 835592 | tf_op jit(solution)/shard_map/ppermute | solution.py:686
  188.6 10.0 %collective-permute-start.27 = (s16[272,512]{1,0:T(8,128)(2,1)S(1)}, s16[272,512]{1,0:T(8,128)(2,1)S(1)}, u32[]{:S(2)}, u32[]{:S(2)}) collective-permute-start(s16[272,512]{1,0:T(8,128)(2,1)S(1)} %code_piece.3.refs_0_), channel_id=1, source_target_pairs={{0,24},{4,28},{8,16},{12,20},{16,8},{20,12},{24,0},{28,4},{1,25},{... | collective-permute-start | bytes 835592 | tf_op jit(solution)/shard_map/ppermute | solution.py:686
  198.7 2.8 %collective-permute-start.28 = (s16[4,272,512]{2,1,0:T(8,128)(2,1)S(1)}, s16[4,272,512]{2,1,0:T(8,128)(2,1)S(1)}, u32[]{:S(2)}, u32[]{:S(2)}) collective-permute-start(s16[4,272,512]{2,1,0:T(8,128)(2,1)S(1)} %lay_coded_pieces.1.mine_ref), channel_id=1, source_target_pairs={{0,4},{4,0},{8,12},{12,8},{16,20},{20,16},{24,28},{28,24},{1,5},{5... | collective-permute-start | bytes 3342344 | tf_op jit(solution)/shard_map/ppermute | solution.py:686
  (22 other events, 121.8 us)

commit v2 on v1

--- a/solution.py
+++ b/solution.py
@@ -642,7 +642,7 @@
             pltpu.SemaphoreType.DMA((layers * (tiles + 5) + 1,)),
             pltpu.SemaphoreType.DMA((layers + 1,)),
         ],
-        compiler_params=pltpu.CompilerParams(vmem_limit_bytes=60 * 1024 * 1024),
+        compiler_params=pltpu.CompilerParams(vmem_limit_bytes=54 * 1024 * 1024),
         name="network_back",
     )(scalars, *sums, *saved, bounds, head_t, kernels_t, mix_t)
 
@@ -743,11 +743,7 @@
         out_ref[place_ref[0] ^ k] = ref[...]
 
 
-def encode_kernel(x_ref, out_ref):
-    encode(x_ref[...], out_ref)
-
-
-def small_call(kernel, name, out_shape, place, *args):
+def small_call(kernel, name, out_shape, place, *args, scratch=()):
     vmem = pl.BlockSpec(memory_space=pltpu.VMEM)
     smem = pl.BlockSpec(memory_space=pltpu.SMEM)
     several = isinstance(out_shape, list)
@@ -757,38 +753,72 @@
         out_shape=out_shape,
         in_specs=[smem] * len(lead) + [vmem] * len(args),
         out_specs=[vmem] * len(out_shape) if several else vmem,
+        scratch_shapes=list(scratch),
         compiler_params=pltpu.CompilerParams(vmem_limit_bytes=32 * 1024 * 1024),
         name=name,
     )(*lead, *args)
 
 
-def scatter_pieces(whole, regions, axis, stride):
-    size = lax.axis_size(axis) // stride
-    place = lax.axis_index(axis) // stride
-    rows, channels = whole.shape[0] // size, whole.shape[1]
-    shapes = [jax.ShapeDtypeStruct((rows, channels), F32)]
-    shapes += [jax.ShapeDtypeStruct((rows + HALO, channels), jnp.int16)] * (size - 1)
-    own, *others = small_call(
-        functools.partial(cut_kernel, size), "cut_pieces", shapes, place, whole, *regions
+def sum_encode_kernel(first_ref, *refs):
+    value = first_ref[...]
+    for ref in refs[:-1]:
+        value = value + decode(ref)
+    encode(value, refs[-1])
+
+
+def sum_cut_kernel(size, count, place_ref, *refs):
+    refs, total = refs[:-1], refs[-1]
+    sum_kernel(*refs[:count], total)
+    cut_kernel(size, place_ref, total, *refs[count:])
+
+
+def lay_encode_kernel(place_ref, *refs):
+    inputs, (out_ref, whole) = refs[:-2], refs[-2:]
+    pieces_kernel(place_ref, *inputs, whole)
+    encode(whole[...], out_ref)
+
+
+def scatter_shapes(rows, channels, size):
+    piece = jax.ShapeDtypeStruct((rows + HALO, channels), jnp.int16)
+    return [jax.ShapeDtypeStruct((rows, channels), F32)] + [piece] * (size - 1)
+
+
+def trade_summands(pieces, axis, stride):
+    return [pieces[0]] + [
+        swap(piece, axis, k * stride) for k, piece in enumerate(pieces) if k
+    ]
+
+
+def sum_coded(kept, sent):
+    chips, freq = lax.axis_size("dp") // 2, lax.axis_size("freq")
+    chip, place = lax.axis_index("dp") // 2, lax.axis_index("freq")
+    channels = kept.shape[1]
+    rows = kept.shape[0] // chips
+    part = rows // freq
+    pieces = small_call(
+        functools.partial(cut_kernel, chips), "cut_pieces", scatter_shapes(rows, channels, chips),
+        chip, kept, swap(sent, "dp", 1),
     )
-    parts = [own] + [swap(piece, axis, (k + 1) * stride) for k, piece in enumerate(others)]
-    return small_call(
-        sum_kernel, "sum_pieces", jax.ShapeDtypeStruct((rows, channels), F32), None, *parts
+    summands = trade_summands(pieces, "dp", 2)
+    pieces = small_call(
+        functools.partial(sum_cut_kernel, freq, chips), "sum_cut_pieces",
+        scatter_shapes(part, channels, freq), place, *summands,
+        scratch=[pltpu.VMEM((rows, channels), F32)],
     )
-
-
-def gather_pieces(x, axis, stride, coded):
-    size = lax.axis_size(axis) // stride
-    place = lax.axis_index(axis) // stride
-    rows, channels = x.shape
-    piece = (rows + HALO, channels)
-    mine = small_call(encode_kernel, "code_piece", jax.ShapeDtypeStruct(piece, jnp.int16), None, x)
-    pieces = [mine] + [swap(mine, axis, k * stride) for k in range(1, size)]
-    if coded:
-        shape = jax.ShapeDtypeStruct((size,) + piece, jnp.int16)
-        return small_call(coded_pieces_kernel, "lay_coded_pieces", shape, place, *pieces)
-    shape = jax.ShapeDtypeStruct((size * rows, channels), F32)
-    return small_call(pieces_kernel, "lay_pieces", shape, place, *pieces)
+    summands = trade_summands(pieces, "freq", 1)
+    mine = small_call(
+        sum_encode_kernel, "sum_code_piece",
+        jax.ShapeDtypeStruct((part + HALO, channels), jnp.int16), None, *summands,
+    )
+    pieces = [mine] + [swap(mine, "freq", k) for k in range(1, freq)]
+    mine = small_call(
+        lay_encode_kernel, "lay_code_piece",
+        jax.ShapeDtypeStruct((rows + HALO, channels), jnp.int16), place, *pieces,
+        scratch=[pltpu.VMEM((rows, channels), F32)],
+    )
+    pieces = [mine] + [swap(mine, "dp", 2 * k) for k in range(1, chips)]
+    shape = jax.ShapeDtypeStruct((chips, rows + HALO, channels), jnp.int16)
+    return small_call(coded_pieces_kernel, "lay_coded_pieces", shape, chip, *pieces)
 
 
 def spread_half(core, coded_ref, half_ref, is_mine, outs, sems):
@@ -838,10 +868,7 @@
 
 def sum_everywhere(kept, sent, sizes, classes):
     core = (lax.axis_index("dp") % 2).reshape(1).astype(jnp.int32)
-    x = scatter_pieces(kept, [swap(sent, "dp", 1)], "dp", 2)
-    x = scatter_pieces(x, [], "freq", 1)
-    x = gather_pieces(x, "freq", 1, False)
-    x = gather_pieces(x, "dp", 2, True)
+    x = sum_coded(kept, sent)
     other = swap(x, "dp", 1)
     channels = x.shape[2]
     shapes = [jax.ShapeDtypeStruct((rows, channels), F32) for rows in sizes[:-1]]

time: 208 us -> 208 us (level)
  no operation moved by 1% of the time
where the time goes in v2:
time: 208 us; the launch traced here: 204 us
  Pallas kernels  91.7 us (44%)
  starting transfers between devices  54.5 us (26%)
  waiting for transfers between devices  42.7 us (21%)
  local copies, waits for them, and re-layouts  12.2 us (6%)
    ppermute x29, starting transfers between devices, swap(): lax.ppermute(x, axis, [(i, i ^ step) for i in range(lax.axis_size(axis))])  54.5 us
    ppermute x29, waiting for transfers between devices, swap(): lax.ppermute(x, axis, [(i, i ^ step) for i in range(lax.axis_size(axis))])  42.7 us
    pallas_call x1, Pallas kernels, network_back(): pl.pallas_call(functools.partial(backward_kernel, count // 32, devices, l...  32 us
    pallas_call x1, Pallas kernels, local(): pl.pallas_call(functools.partial(forward_kernel, run, freq, chunks), out_...  17.6 us
    pallas_call x2, Pallas kernels, first_section(): pl.pallas_call(functools.partial(first_kernel, devices), out_shape=[jax.S...  17.4 us
    pallas_call x2, Pallas kernels, second_section(): pl.pallas_call(functools.partial(second_kernel, devices, total_len), out_...  16.4 us
    unnamed x50, local copies, waits for them, and re-layouts  11.2 us
  transfers between devices with their start and end apart: 29, of which 15 were waited for; matrix products, arithmetic and copies ran while one was open for 1% of the time, Pallas kernels for 14%

profile of v2, /device:TPU:0, one launch (start us, length us, event | category | flops | bytes accessed | tf_op | source)
XLA Modules:
  0.0 204.1 jit_solution(4647195462546104631)
XLA Ops:
  0.6 8.6 %first_section.2 = (s16[528,256]{1,0:T(8,128)(2,1)}, s16[528,256]{1,0:T(8,128)(2,1)}, s16[528,256]{1,0:T(8,128)(2,1)}, s16[528,256]{1,0:T(8,128)(2,1)}) custom-call(s32[1]{0:T(128)} %bitcast.2.place_ref, f32[2,1024,512]{2,1,0:T(8,128)} %bitcast.9, bf16[2,1024,1024]{2,1,0:T(8,128)(2,1)} %constant.63.clone.table_ref, f32[2048,1024]{1,0:T(8,128)} %constant.64.clone.twiddle_ref), custom_call_target="tpu_custom_call" | custom-call | flops 3221225472 | bytes 8388608 | tf_op jit(solution)/shard_map/first_section/pallas_call | solution.py:107
  9.3 3.0 %collective-permute-start = (s16[528,256]{1,0:T(8,128)(2,1)}, s16[528,256]{1,0:T(8,128)(2,1)S(1)}, u32[]{:S(2)}, u32[]{:S(2)}) collective-permute-start(s16[528,256]{1,0:T(8,128)(2,1)} %get-tuple-element.55), channel_id=1, source_target_pairs={{0,1},{1,0},{2,3},{3,2},{4,5},{5,4},{6,7},{7,6},{8,9},{9,8},{10,11... | collective-permute-start | bytes 811016 | tf_op jit(solution)/shard_map/ppermute | solution.py:686
  12.3 2.6 %collective-permute-start.1 = (s16[528,256]{1,0:T(8,128)(2,1)}, s16[528,256]{1,0:T(8,128)(2,1)S(1)}, u32[]{:S(2)}, u32[]{:S(2)}) collective-permute-start(s16[528,256]{1,0:T(8,128)(2,1)} %get-tuple-element.56), channel_id=1, source_target_pairs={{0,2},{1,3},{2,0},{3,1},{4,6},{5,7},{6,4},{7,5},{8,10},{9,11},{10,... | collective-permute-start | bytes 811016 | tf_op jit(solution)/shard_map/ppermute | solution.py:686
  15.0 8.7 %first_section.3 = (s16[528,256]{1,0:T(8,128)(2,1)}, s16[528,256]{1,0:T(8,128)(2,1)}, s16[528,256]{1,0:T(8,128)(2,1)}, s16[528,256]{1,0:T(8,128)(2,1)}) custom-call(s32[1]{0:T(128)} %bitcast.2.place_ref, f32[2,1024,512]{2,1,0:T(8,128)} %bitcast.10, bf16[2,1024,1024]{2,1,0:T(8,128)(2,1)} %constant.63.clone.table_ref, f32[2048,1024]{1,0:T(8,128)} %constant.64.clone.twiddle_ref), custom_call_target="tpu_custom_call" | custom-call | flops 3221225472 | bytes 8388608 | tf_op jit(solution)/shard_map/first_section/pallas_call | solution.py:107
  24.6 3.4 %collective-permute-start.7 = (s16[528,256]{1,0:T(8,128)(2,1)}, s16[528,256]{1,0:T(8,128)(2,1)S(1)}, u32[]{:S(2)}, u32[]{:S(2)}) collective-permute-start(s16[528,256]{1,0:T(8,128)(2,1)} %get-tuple-element.71), channel_id=1, source_target_pairs={{0,2},{1,3},{2,0},{3,1},{4,6},{5,7},{6,4},{7,5},{8,10},{9,11},{10,... | collective-permute-start | bytes 811016 | tf_op jit(solution)/shard_map/ppermute | solution.py:686
  28.0 1.5 dense_weights.1
  34.5 1.6 copy-done.10
  37.5 8.2 %second_section.2 = (bf16[528,128]{1,0:T(8,128)(2,1)S(1)}, bf16[528,128]{1,0:T(8,128)(2,1)S(1)}, bf16[528,128]{1,0:T(8,128)(2,1)S(1)}, bf16[528,128]{1,0:T(8,128)(2,1)S(1)}) custom-call(s32[1]{0:T(128)} %bitcast.2.place_ref, s16[528,256]{1,0:T(8,128)(2,1)S(1)} %copy-done.9, s16[528,256]{1,0:T(8,128)(2,1)S(1)} %collective-permute-done.refs_1_, ...), custom_call_target="tpu_custom_call" | custom-call | flops 3221225472 | bytes 8388608 | tf_op jit(solution)/shard_map/second_section/pallas_call | solution.py:212
  46.3 17.9 %collective-permute-start.3 = (bf16[528,128]{1,0:T(8,128)(2,1)S(1)}, bf16[528,128]{1,0:T(8,128)(2,1)S(1)}, u32[]{:S(2)}, u32[]{:S(2)}) collective-permute-start(bf16[528,128]{1,0:T(8,128)(2,1)S(1)} %get-tuple-element.66), channel_id=1, source_target_pairs={{0,1},{1,0},{2,3},{3,2},{4,5},{5,4},{6,7},{7,6},{8,9},{9,8},{10,11... | collective-permute-start | bytes 405512 | tf_op jit(solution)/shard_map/ppermute | solution.py:686
  66.8 8.2 %second_section.3 = (bf16[528,128]{1,0:T(8,128)(2,1)S(1)}, bf16[528,128]{1,0:T(8,128)(2,1)S(1)}, bf16[528,128]{1,0:T(8,128)(2,1)S(1)}, bf16[528,128]{1,0:T(8,128)(2,1)S(1)}) custom-call(s32[1]{0:T(128)} %bitcast.2.place_ref, s16[528,256]{1,0:T(8,128)(2,1)S(1)} %copy-done.8, s16[528,256]{1,0:T(8,128)(2,1)S(1)} %collective-permute-done.6.refs_1_, ...), custom_call_target="tpu_custom_call" | custom-call | flops 3221225472 | bytes 8388608 | tf_op jit(solution)/shard_map/second_section/pallas_call | solution.py:212
  75.7 2.0 collective-permute-start.10
  80.8 4.3 %collective-permute-done.10.refs_6_ = bf16[528,128]{1,0:T(8,128)(2,1)S(1)} collective-permute-done((bf16[528,128]{1,0:T(8,128)(2,1)S(1)}, bf16[528,128]{1,0:T(8,128)(2,1)S(1)}, u32[]{:S(2)}, u32[]{:S(2)}) %collective-permute-start.10) | collective-permute-done | bytes 135200 | tf_op jit(solution)/shard_map/ppermute | solution.py:686
  87.1 17.6 %network_ahead.1 = (f32[3,2064,512]{2,1,0:T(8,128)}, f32[3,2064,128]{2,1,0:T(8,128)}, bf16[3,2192,512]{2,1,0:T(8,128)(2,1)}, bf16[2064,256]{1,0:T(8,128)(2,1)}, f32[8,512]{1,0:T(8,128)}) custom-call(s32[1]{0:T(128)} %bitcast.2.place_ref, bf16[528,128]{1,0:T(8,128)(2,1)} %copy-done.6, bf16[528,128]{1,0:T(8,128)(2,1)} %copy-done.14, ...), custom_call_target="tpu_custom_call" | custom-call | tf_op jit(solution)/shard_map/network_ahead/pallas_call | solution.py:949
  105.5 1.8 collective-permute-start.13
  107.3 1.8 collective-permute-start.14
  110.4 2.7 %collective-permute-done.14.refs_3_ = f32[8,512]{1,0:T(8,128)S(1)} collective-permute-done((f32[8,512]{1,0:T(8,128)}, f32[8,512]{1,0:T(8,128)S(1)}, u32[]{:S(2)}, u32[]{:S(2)}) %collective-permute-start.14) | collective-permute-done | bytes 16416 | tf_op jit(solution)/shard_map/ppermute | solution.py:686
  113.7 32.0 %network_back.1 = (f32[1024,512]{1,0:T(8,128)}, s16[2,528,512]{2,1,0:T(8,128)(2,1)}) custom-call(s32[4]{0:T(128)} %pad_add_fusion.1.place_ref, f32[8,512]{1,0:T(8,128)} %get-tuple-element.78.refs_0_, f32[8,512]{1,0:T(8,128)} %copy-done.21, f32[8,512]{1,0:T(8,128)} %copy-done.22, f32[8,512]{1,0:T(8,128)} %copy-done.23, ...), custom_call_target="tpu_custom_call" | custom-call | tf_op jit(solution)/shard_map/network_back/pallas_call | solution.py:620
  145.8 2.9 %collective-permute-done.15.refs_0_ = s16[2,528,512]{2,1,0:T(8,128)(2,1)S(1)} collective-permute-done((s16[2,528,512]{2,1,0:T(8,128)(2,1)}, s16[2,528,512]{2,1,0:T(8,128)(2,1)S(1)}, u32[]{:S(2)}, u32[]{:S(2)}) %collective-permute-start.15) | collective-permute-done | bytes 1081376 | tf_op jit(solution)/shard_map/ppermute | solution.py:686
  148.7 1.6 copy-done.3
  151.4 1.5 collective-permute-start.16
  153.0 1.5 collective-permute-start.17
  155.0 6.0 %collective-permute-done.16.refs_1_ = s16[272,512]{1,0:T(8,128)(2,1)S(1)} collective-permute-done((s16[272,512]{1,0:T(8,128)(2,1)S(1)}, s16[272,512]{1,0:T(8,128)(2,1)S(1)}, u32[]{:S(2)}, u32[]{:S(2)}) %collective-permute-start.16) | collective-permute-done | bytes 278560 | tf_op jit(solution)/shard_map/ppermute | solution.py:686
  161.0 6.4 %collective-permute-done.17.refs_2_ = s16[272,512]{1,0:T(8,128)(2,1)S(1)} collective-permute-done((s16[272,512]{1,0:T(8,128)(2,1)S(1)}, s16[272,512]{1,0:T(8,128)(2,1)S(1)}, u32[]{:S(2)}, u32[]{:S(2)}) %collective-permute-start.17) | collective-permute-done | bytes 278560 | tf_op jit(solution)/shard_map/ppermute | solution.py:686
  168.0 2.4 %collective-permute-start.20 = (s16[80,512]{1,0:T(8,128)(2,1)S(1)}, s16[80,512]{1,0:T(8,128)(2,1)S(1)}, u32[]{:S(2)}, u32[]{:S(2)}) collective-permute-start(s16[80,512]{1,0:T(8,128)(2,1)S(1)} %get-tuple-element.93), channel_id=1, source_target_pairs={{0,2},{1,3},{2,0},{3,1},{4,6},{5,7},{6,4},{7,5},{8,10},{9,11},{10,... | collective-permute-start | bytes 245768 | tf_op jit(solution)/shard_map/ppermute | solution.py:686
  170.5 1.9 collective-permute-start.21
  172.4 4.4 %collective-permute-done.20.refs_1_ = s16[80,512]{1,0:T(8,128)(2,1)S(1)} collective-permute-done((s16[80,512]{1,0:T(8,128)(2,1)S(1)}, s16[80,512]{1,0:T(8,128)(2,1)S(1)}, u32[]{:S(2)}, u32[]{:S(2)}) %collective-permute-start.20) | collective-permute-done | bytes 81952 | tf_op jit(solution)/shard_map/ppermute | solution.py:686
  179.7 1.9 collective-permute-start.24
  182.9 2.0 collective-permute-done.23.refs_2_
  190.0 4.2 %collective-permute-done.25.refs_1_ = s16[272,512]{1,0:T(8,128)(2,1)S(1)} collective-permute-done((s16[272,512]{1,0:T(8,128)(2,1)S(1)}, s16[272,512]{1,0:T(8,128)(2,1)S(1)}, u32[]{:S(2)}, u32[]{:S(2)}) %collective-permute-start.25) | collective-permute-done | bytes 278560 | tf_op jit(solution)/shard_map/ppermute | solution.py:686
  194.2 4.4 %collective-permute-done.26.refs_2_ = s16[272,512]{1,0:T(8,128)(2,1)S(1)} collective-permute-done((s16[272,512]{1,0:T(8,128)(2,1)S(1)}, s16[272,512]{1,0:T(8,128)(2,1)S(1)}, u32[]{:S(2)}, u32[]{:S(2)}) %collective-permute-start.26) | collective-permute-done | bytes 278560 | tf_op jit(solution)/shard_map/ppermute | solution.py:686
  198.7 1.8 spread_mine.1
  201.5 2.4 %spread_other.1 = (f32[1536,512]{1,0:T(8,128)}, f32[256,512]{1,0:T(8,128)}, f32[144,512]{1,0:T(8,128)}, f32[10,512]{1,0:T(8,128)}, f32[1,1]{1,0:T(1,128)}) custom-call(s32[1]{0:T(128)} %bitcast.core_ref, s16[4,272,512]{2,1,0:T(8,128)(2,1)S(1)} %lay_coded_pieces.1.mine_ref, ...), custom_call_target="tpu_custom_call", output_to_operand_aliasing={{0}: (3, {}), {1}: (4, {}), {2}: (5, {})} | custom-call | tf_op jit(solution)/shard_map/spread_other/pallas_call | solution.py:889
  (99 shorter events, 30.9 us)
Async XLA Ops:
  9.3 24.3 %collective-permute-start = (s16[528,256]{1,0:T(8,128)(2,1)}, s16[528,256]{1,0:T(8,128)(2,1)S(1)}, u32[]{:S(2)}, u32[]{:S(2)}) collective-permute-start(s16[528,256]{1,0:T(8,128)(2,1)} %get-tuple-element.55), channel_id=1, source_target_pairs={{0,1},{1,0},{2,3},{3,2},{4,5},{5,4},{6,7},{7,6},{8,9},{9,8},{10,11... | collective-permute-start | bytes 811016 | tf_op jit(solution)/shard_map/ppermute | solution.py:686
  12.3 22.1 %collective-permute-start.1 = (s16[528,256]{1,0:T(8,128)(2,1)}, s16[528,256]{1,0:T(8,128)(2,1)S(1)}, u32[]{:S(2)}, u32[]{:S(2)}) collective-permute-start(s16[528,256]{1,0:T(8,128)(2,1)} %get-tuple-element.56), channel_id=1, source_target_pairs={{0,2},{1,3},{2,0},{3,1},{4,6},{5,7},{6,4},{7,5},{8,10},{9,11},{10,... | collective-permute-start | bytes 811016 | tf_op jit(solution)/shard_map/ppermute | solution.py:686
  14.9 19.5 %collective-permute-start.2 = (s16[528,256]{1,0:T(8,128)(2,1)}, s16[528,256]{1,0:T(8,128)(2,1)S(1)}, u32[]{:S(2)}, u32[]{:S(2)}) collective-permute-start(s16[528,256]{1,0:T(8,128)(2,1)} %get-tuple-element.57), channel_id=1, source_target_pairs={{0,3},{1,2},{2,1},{3,0},{4,7},{5,6},{6,5},{7,4},{8,11},{9,10},{10,... | collective-permute-start | bytes 811016 | tf_op jit(solution)/shard_map/ppermute | solution.py:686
  23.7 41.6 %collective-permute-start.6 = (s16[528,256]{1,0:T(8,128)(2,1)}, s16[528,256]{1,0:T(8,128)(2,1)S(1)}, u32[]{:S(2)}, u32[]{:S(2)}) collective-permute-start(s16[528,256]{1,0:T(8,128)(2,1)} %get-tuple-element.70), channel_id=1, source_target_pairs={{0,1},{1,0},{2,3},{3,2},{4,5},{5,4},{6,7},{7,6},{8,9},{9,8},{10,11... | collective-permute-start | bytes 811016 | tf_op jit(solution)/shard_map/ppermute | solution.py:686
  24.6 42.2 %collective-permute-start.7 = (s16[528,256]{1,0:T(8,128)(2,1)}, s16[528,256]{1,0:T(8,128)(2,1)S(1)}, u32[]{:S(2)}, u32[]{:S(2)}) collective-permute-start(s16[528,256]{1,0:T(8,128)(2,1)} %get-tuple-element.71), channel_id=1, source_target_pairs={{0,2},{1,3},{2,0},{3,1},{4,6},{5,7},{6,4},{7,5},{8,10},{9,11},{10,... | collective-permute-start | bytes 811016 | tf_op jit(solution)/shard_map/ppermute | solution.py:686
  33.6 33.2 %collective-permute-start.8 = (s16[528,256]{1,0:T(8,128)(2,1)}, s16[528,256]{1,0:T(8,128)(2,1)S(1)}, u32[]{:S(2)}, u32[]{:S(2)}) collective-permute-start(s16[528,256]{1,0:T(8,128)(2,1)} %get-tuple-element.72), channel_id=1, source_target_pairs={{0,3},{1,2},{2,1},{3,0},{4,7},{5,6},{6,5},{7,4},{8,11},{9,10},{10,... | collective-permute-start | bytes 811016 | tf_op jit(solution)/shard_map/ppermute | solution.py:686
  37.5 29.3 %copy-start.8 = (s16[528,256]{1,0:T(8,128)(2,1)S(1)}, s16[528,256]{1,0:T(8,128)(2,1)}, u32[]{:S(2)}) copy-start(s16[528,256]{1,0:T(8,128)(2,1)} %get-tuple-element.69.refs_0_) | copy-start | bytes 811012
  37.5 29.3 %copy-start.11 = (bf16[2,512,1024]{2,1,0:T(8,128)(2,1)S(1)}, bf16[2,512,1024]{2,1,0:T(8,128)(2,1)}, u32[]{:S(2)}) copy-start(bf16[2,512,1024]{2,1,0:T(8,128)(2,1)} %constant.66.clone.refs_5_) | copy-start | bytes 6291460
  46.3 32.7 %collective-permute-start.3 = (bf16[528,128]{1,0:T(8,128)(2,1)S(1)}, bf16[528,128]{1,0:T(8,128)(2,1)S(1)}, u32[]{:S(2)}, u32[]{:S(2)}) collective-permute-start(bf16[528,128]{1,0:T(8,128)(2,1)S(1)} %get-tuple-element.66), channel_id=1, source_target_pairs={{0,1},{1,0},{2,3},{3,2},{4,5},{5,4},{6,7},{7,6},{8,9},{9,8},{10,11... | collective-permute-start | bytes 405512 | tf_op jit(solution)/shard_map/ppermute | solution.py:686
  64.3 16.5 %collective-permute-start.4 = (bf16[528,128]{1,0:T(8,128)(2,1)S(1)}, bf16[528,128]{1,0:T(8,128)(2,1)S(1)}, u32[]{:S(2)}, u32[]{:S(2)}) collective-permute-start(bf16[528,128]{1,0:T(8,128)(2,1)S(1)} %get-tuple-element.67), channel_id=1, source_target_pairs={{0,2},{1,3},{2,0},{3,1},{4,6},{5,7},{6,4},{7,5},{8,10},{9,11},{10,... | collective-permute-start | bytes 405512 | tf_op jit(solution)/shard_map/ppermute | solution.py:686
  65.3 15.5 %collective-permute-start.5 = (bf16[528,128]{1,0:T(8,128)(2,1)S(1)}, bf16[528,128]{1,0:T(8,128)(2,1)S(1)}, u32[]{:S(2)}, u32[]{:S(2)}) collective-permute-start(bf16[528,128]{1,0:T(8,128)(2,1)S(1)} %get-tuple-element.68), channel_id=1, source_target_pairs={{0,3},{1,2},{2,1},{3,0},{4,7},{5,6},{6,5},{7,4},{8,11},{9,10},{10,... | collective-permute-start | bytes 405512 | tf_op jit(solution)/shard_map/ppermute | solution.py:686
  75.7 9.5 %collective-permute-start.10 = (bf16[528,128]{1,0:T(8,128)(2,1)S(1)}, bf16[528,128]{1,0:T(8,128)(2,1)S(1)}, u32[]{:S(2)}, u32[]{:S(2)}) collective-permute-start(bf16[528,128]{1,0:T(8,128)(2,1)S(1)} %get-tuple-element.75), channel_id=1, source_target_pairs={{0,2},{1,3},{2,0},{3,1},{4,6},{5,7},{6,4},{7,5},{8,10},{9,11},{10,... | collective-permute-start | bytes 405512 | tf_op jit(solution)/shard_map/ppermute | solution.py:686
  77.7 7.5 %collective-permute-start.11 = (bf16[528,128]{1,0:T(8,128)(2,1)S(1)}, bf16[528,128]{1,0:T(8,128)(2,1)S(1)}, u32[]{:S(2)}, u32[]{:S(2)}) collective-permute-start(bf16[528,128]{1,0:T(8,128)(2,1)S(1)} %get-tuple-element.76), channel_id=1, source_target_pairs={{0,3},{1,2},{2,1},{3,0},{4,7},{5,6},{6,5},{7,4},{8,11},{9,10},{10,... | collective-permute-start | bytes 405512 | tf_op jit(solution)/shard_map/ppermute | solution.py:686
  79.1 7.4 %collective-permute-start.9 = (bf16[528,128]{1,0:T(8,128)(2,1)S(1)}, bf16[528,128]{1,0:T(8,128)(2,1)S(1)}, u32[]{:S(2)}, u32[]{:S(2)}) collective-permute-start(bf16[528,128]{1,0:T(8,128)(2,1)S(1)} %get-tuple-element.74), channel_id=1, source_target_pairs={{0,1},{1,0},{2,3},{3,2},{4,5},{5,4},{6,7},{7,6},{8,9},{9,8},{10,11... | collective-permute-start | bytes 405512 | tf_op jit(solution)/shard_map/ppermute | solution.py:686
  87.1 22.6 %copy-start.20 = (f32[512,10]{0,1:T(8,128)S(1)}, f32[512,10]{0,1:T(8,128)}, u32[]{:S(2)}) copy-start(f32[512,10]{0,1:T(8,128)} %param.16) | copy-start | bytes 61444
  104.7 5.7 %collective-permute-start.12 = (f32[8,512]{1,0:T(8,128)}, f32[8,512]{1,0:T(8,128)S(1)}, u32[]{:S(2)}, u32[]{:S(2)}) collective-permute-start(f32[8,512]{1,0:T(8,128)} %get-tuple-element.78.refs_0_), channel_id=1, source_target_pairs={{0,1},{1,0},{2,3},{3,2},{4,5},{5,4},{6,7},{7,6},{8,9},{9,8},{10,11... | collective-permute-start | bytes 49160 | tf_op jit(solution)/shard_map/ppermute | solution.py:686
  105.5 4.9 %collective-permute-start.13 = (f32[8,512]{1,0:T(8,128)}, f32[8,512]{1,0:T(8,128)S(1)}, u32[]{:S(2)}, u32[]{:S(2)}) collective-permute-start(f32[8,512]{1,0:T(8,128)} %get-tuple-element.78.refs_0_), channel_id=1, source_target_pairs={{0,2},{1,3},{2,0},{3,1},{4,6},{5,7},{6,4},{7,5},{8,10},{9,11},{10,... | collective-permute-start | bytes 49160 | tf_op jit(solution)/shard_map/ppermute | solution.py:686
  107.3 5.7 %collective-permute-start.14 = (f32[8,512]{1,0:T(8,128)}, f32[8,512]{1,0:T(8,128)S(1)}, u32[]{:S(2)}, u32[]{:S(2)}) collective-permute-start(f32[8,512]{1,0:T(8,128)} %get-tuple-element.78.refs_0_), channel_id=1, source_target_pairs={{0,3},{1,2},{2,1},{3,0},{4,7},{5,6},{6,5},{7,4},{8,11},{9,10},{10,... | collective-permute-start | bytes 49160 | tf_op jit(solution)/shard_map/ppermute | solution.py:686
  145.7 3.0 %collective-permute-start.15 = (s16[2,528,512]{2,1,0:T(8,128)(2,1)}, s16[2,528,512]{2,1,0:T(8,128)(2,1)S(1)}, u32[]{:S(2)}, u32[]{:S(2)}) collective-permute-start(s16[2,528,512]{2,1,0:T(8,128)(2,1)} %get-tuple-element.86), channel_id=1, source_target_pairs={{0,4},{4,0},{8,12},{12,8},{16,20},{20,16},{24,28},{28,24},{1,5},{5... | collective-permute-start | bytes 3244040 | tf_op jit(solution)/shard_map/ppermute | solution.py:686
  151.4 9.5 %collective-permute-start.16 = (s16[272,512]{1,0:T(8,128)(2,1)S(1)}, s16[272,512]{1,0:T(8,128)(2,1)S(1)}, u32[]{:S(2)}, u32[]{:S(2)}) collective-permute-start(s16[272,512]{1,0:T(8,128)(2,1)S(1)} %get-tuple-element.88), channel_id=1, source_target_pairs={{0,8},{4,12},{8,0},{12,4},{16,24},{20,28},{24,16},{28,20},{1,9},{5... | collective-permute-start | bytes 835592 | tf_op jit(solution)/shard_map/ppermute | solution.py:686
  153.0 14.4 %collective-permute-start.17 = (s16[272,512]{1,0:T(8,128)(2,1)S(1)}, s16[272,512]{1,0:T(8,128)(2,1)S(1)}, u32[]{:S(2)}, u32[]{:S(2)}) collective-permute-start(s16[272,512]{1,0:T(8,128)(2,1)S(1)} %get-tuple-element.89), channel_id=1, source_target_pairs={{0,16},{4,20},{8,24},{12,28},{16,0},{20,4},{24,8},{28,12},{1,17},{... | collective-permute-start | bytes 835592 | tf_op jit(solution)/shard_map/ppermute | solution.py:686
  154.5 12.9 %collective-permute-start.18 = (s16[272,512]{1,0:T(8,128)(2,1)S(1)}, s16[272,512]{1,0:T(8,128)(2,1)S(1)}, u32[]{:S(2)}, u32[]{:S(2)}) collective-permute-start(s16[272,512]{1,0:T(8,128)(2,1)S(1)} %get-tuple-element.90), channel_id=1, source_target_pairs={{0,24},{4,28},{8,16},{12,20},{16,8},{20,12},{24,0},{28,4},{1,25},{... | collective-permute-start | bytes 835592 | tf_op jit(solution)/shard_map/ppermute | solution.py:686
  168.0 4.5 %collective-permute-start.19 = (s16[80,512]{1,0:T(8,128)(2,1)S(1)}, s16[80,512]{1,0:T(8,128)(2,1)S(1)}, u32[]{:S(2)}, u32[]{:S(2)}) collective-permute-start(s16[80,512]{1,0:T(8,128)(2,1)S(1)} %get-tuple-element.92), channel_id=1, source_target_pairs={{0,1},{1,0},{2,3},{3,2},{4,5},{5,4},{6,7},{7,6},{8,9},{9,8},{10,11... | collective-permute-start | bytes 245768 | tf_op jit(solution)/shard_map/ppermute | solution.py:686
  168.0 8.8 %collective-permute-start.20 = (s16[80,512]{1,0:T(8,128)(2,1)S(1)}, s16[80,512]{1,0:T(8,128)(2,1)S(1)}, u32[]{:S(2)}, u32[]{:S(2)}) collective-permute-start(s16[80,512]{1,0:T(8,128)(2,1)S(1)} %get-tuple-element.93), channel_id=1, source_target_pairs={{0,2},{1,3},{2,0},{3,1},{4,6},{5,7},{6,4},{7,5},{8,10},{9,11},{10,... | collective-permute-start | bytes 245768 | tf_op jit(solution)/shard_map/ppermute | solution.py:686
  170.5 6.4 %collective-permute-start.21 = (s16[80,512]{1,0:T(8,128)(2,1)S(1)}, s16[80,512]{1,0:T(8,128)(2,1)S(1)}, u32[]{:S(2)}, u32[]{:S(2)}) collective-permute-start(s16[80,512]{1,0:T(8,128)(2,1)S(1)} %get-tuple-element.94), channel_id=1, source_target_pairs={{0,3},{1,2},{2,1},{3,0},{4,7},{5,6},{6,5},{7,4},{8,11},{9,10},{10,... | collective-permute-start | bytes 245768 | tf_op jit(solution)/shard_map/ppermute | solution.py:686
  177.2 5.7 %collective-permute-start.22 = (s16[80,512]{1,0:T(8,128)(2,1)S(1)}, s16[80,512]{1,0:T(8,128)(2,1)S(1)}, u32[]{:S(2)}, u32[]{:S(2)}) collective-permute-start(s16[80,512]{1,0:T(8,128)(2,1)S(1)} %sum_code_piece.1.refs_0_), channel_id=1, source_target_pairs={{0,1},{1,0},{2,3},{3,2},{4,5},{5,4},{6,7},{7,6},{8,9},{9,8},{10,11... | collective-permute-start | bytes 245768 | tf_op jit(solution)/shard_map/ppermute | solution.py:686
  178.6 6.2 %collective-permute-start.23 = (s16[80,512]{1,0:T(8,128)(2,1)S(1)}, s16[80,512]{1,0:T(8,128)(2,1)S(1)}, u32[]{:S(2)}, u32[]{:S(2)}) collective-permute-start(s16[80,512]{1,0:T(8,128)(2,1)S(1)} %sum_code_piece.1.refs_0_), channel_id=1, source_target_pairs={{0,2},{1,3},{2,0},{3,1},{4,6},{5,7},{6,4},{7,5},{8,10},{9,11},{10,... | collective-permute-start | bytes 245768 | tf_op jit(solution)/shard_map/ppermute | solution.py:686
  179.7 6.3 %collective-permute-start.24 = (s16[80,512]{1,0:T(8,128)(2,1)S(1)}, s16[80,512]{1,0:T(8,128)(2,1)S(1)}, u32[]{:S(2)}, u32[]{:S(2)}) collective-permute-start(s16[80,512]{1,0:T(8,128)(2,1)S(1)} %sum_code_piece.1.refs_0_), channel_id=1, source_target_pairs={{0,3},{1,2},{2,1},{3,0},{4,7},{5,6},{6,5},{7,4},{8,11},{9,10},{10,... | collective-permute-start | bytes 245768 | tf_op jit(solution)/shard_map/ppermute | solution.py:686
  186.5 7.7 %collective-permute-start.25 = (s16[272,512]{1,0:T(8,128)(2,1)S(1)}, s16[272,512]{1,0:T(8,128)(2,1)S(1)}, u32[]{:S(2)}, u32[]{:S(2)}) collective-permute-start(s16[272,512]{1,0:T(8,128)(2,1)S(1)} %lay_code_piece.1.refs_0_), channel_id=1, source_target_pairs={{0,8},{4,12},{8,0},{12,4},{16,24},{20,28},{24,16},{28,20},{1,9},{5... | collective-permute-start | bytes 835592 | tf_op jit(solution)/shard_map/ppermute | solution.py:686
  187.9 10.7 %collective-permute-start.26 = (s16[272,512]{1,0:T(8,128)(2,1)S(1)}, s16[272,512]{1,0:T(8,128)(2,1)S(1)}, u32[]{:S(2)}, u32[]{:S(2)}) collective-permute-start(s16[272,512]{1,0:T(8,128)(2,1)S(1)} %lay_code_piece.1.refs_0_), channel_id=1, source_target_pairs={{0,16},{4,20},{8,24},{12,28},{16,0},{20,4},{24,8},{28,12},{1,17},{... | collective-permute-start | bytes 835592 | tf_op jit(solution)/shard_map/ppermute | solution.py:686
  188.6 10.0 %collective-permute-start.27 = (s16[272,512]{1,0:T(8,128)(2,1)S(1)}, s16[272,512]{1,0:T(8,128)(2,1)S(1)}, u32[]{:S(2)}, u32[]{:S(2)}) collective-permute-start(s16[272,512]{1,0:T(8,128)(2,1)S(1)} %lay_code_piece.1.refs_0_), channel_id=1, source_target_pairs={{0,24},{4,28},{8,16},{12,20},{16,8},{20,12},{24,0},{28,4},{1,25},{... | collective-permute-start | bytes 835592 | tf_op jit(solution)/shard_map/ppermute | solution.py:686
  198.7 2.8 %collective-permute-start.28 = (s16[4,272,512]{2,1,0:T(8,128)(2,1)S(1)}, s16[4,272,512]{2,1,0:T(8,128)(2,1)S(1)}, u32[]{:S(2)}, u32[]{:S(2)}) collective-permute-start(s16[4,272,512]{2,1,0:T(8,128)(2,1)S(1)} %lay_coded_pieces.1.mine_ref), channel_id=1, source_target_pairs={{0,4},{4,0},{8,12},{12,8},{16,20},{20,16},{24,28},{28,24},{1,5},{5... | collective-permute-start | bytes 3342344 | tf_op jit(solution)/shard_map/ppermute | solution.py:686
  (22 other events, 121.8 us)
